TPU v7x, 32 devices: a whole 2x2x4 slice. The times are simulated.
32 devices in a mesh: row: 8 (over z, y), band: 4 (over x, core).
Axes of the slice: x: 2, y: 2, z: 4, core: 2. Of those that a mesh axis runs over, the one named last changes fastest.
Arguments:
- nodes: float32 [8, 3, 512], P('row', None, 'band'), may hold values from -6 to 6
- segments: float32 [8, 6, 3072], P('row', None, 'band'), may hold values from -6 to 6
- circulation: float32 [8, 3072], P('row', 'band'), may hold values from -1 to 1
- upstream: int32 [8, 3], P('row'), may hold values from 0 to 3, as said below
- upstream_mask: int32 [8, 3], P('row'), may hold values from 0 to 1, as said below
Outputs:
- new_nodes: float32 [8, 3, 512], P('row', None, 'band')
- velocity_first: float32 [8, 3, 512], P('row', None, 'band')
Inputs may be any that keep to these rules, and one draw needn't show every extreme that they name: `upstream`: each turbine's used entries come first and name distinct turbines of the previous downwind row of 4 turbines (turbine t lies in downwind row t // 4); unused entries are 0. `upstream_mask`: turbines of the first downwind row use no entries; the last turbine uses all three.
All inputs are finite; a program needn't handle non-finite values.
Results may differ from a plain program's by a relative error of at most 0.00014.
Values sent between devices are 32-bit elements; how exact they have to be, the bound alone decides.
No kernel may reach another device: no remote copies, remote signals or barrier semaphores. Data moves between devices by JAX's collectives and lax.ppermute only.
A program may use at most 64 MiB of HBM per device.

v0:
```python
import math

import jax
import jax.numpy as jnp
from jax import lax
from jax.sharding import PartitionSpec as P

FIL = 8


CORE_SQUARE = 0.04
AGE_STEP = 0.25


def passed_along(block, axis, distance):
    devices = range(lax.axis_size(axis))
    route = [(i - distance, i) for i in devices if i - distance in devices]
    return lax.ppermute(block, axis, route)


def segment_piece(points, piece):
    rel_one = points[:, :, None] - piece[0:3, None, :]
    rel_two = points[:, :, None] - piece[3:6, None, :]
    cross_x = rel_one[1] * rel_two[2] - rel_one[2] * rel_two[1]
    cross_y = rel_one[2] * rel_two[0] - rel_one[0] * rel_two[2]
    cross_z = rel_one[0] * rel_two[1] - rel_one[1] * rel_two[0]
    norm_one = jnp.sqrt(jnp.sum(rel_one * rel_one, axis=0) + CORE_SQUARE)
    norm_two = jnp.sqrt(jnp.sum(rel_two * rel_two, axis=0) + CORE_SQUARE)
    inner = jnp.sum(rel_one * rel_two, axis=0)
    product = norm_one * norm_two
    factor = (
        piece[6][None, :] * (norm_one + norm_two) / (4.0 * math.pi * product * (product + inner))
    )
    return jnp.stack(
        [
            jnp.sum(cross_x * factor, axis=1),
            jnp.sum(cross_y * factor, axis=1),
            jnp.sum(cross_z * factor, axis=1),
        ]
    )


def induce(points, block):
    columns = block.shape[1]
    piece_len = 256
    pieces = block.reshape(7, columns // piece_len, piece_len).transpose(1, 0, 2)

    def accumulate(total, piece):
        return (total + segment_piece(points, piece), None)

    total, ignored = lax.scan(accumulate, jnp.zeros((3, points.shape[1]), jnp.float32), pieces)
    return total


def free_stream():
    return jnp.array([1.0, 0.0, 0.0], jnp.float32)[:, None]


def upstream_reach():
    return 2 * min(8, lax.axis_size("row") // 2) - 1


def local(nodes, segments, circulation, upstream, upstream_mask):
    turbine = lax.axis_index("row")
    band_index = lax.axis_index("band")
    reach = upstream_reach()
    points = nodes[0]
    listed = upstream[0]
    active = upstream_mask[0] > 0
    own_block = jnp.concatenate([segments[0], circulation[0][None, :]], axis=0)

    def velocity(where_at):
        targets = lax.all_gather(where_at, "band", axis=1, tiled=True)
        total = induce(targets, own_block)

        def one_hop(offset, state):
            block, running = state
            block = passed_along(block, "row", 1)
            source = turbine - offset - 1
            matched = jnp.any((listed == source) & active)
            running = lax.cond(
                matched, lambda value: value + induce(targets, block), lambda value: value, running
            )
            return (block, running)

        ignored, total = lax.fori_loop(0, reach, one_hop, (own_block, total))
        total = lax.psum_scatter(total, "band", scatter_dimension=1, tiled=True)
        return total + free_stream()

    first = velocity(points)
    rim_data = passed_along(
        jnp.concatenate([points[:, -2 * FIL :], first[:, -FIL:]], axis=1), "band", 1
    )
    at_start = band_index == 0
    root_pair = jnp.concatenate([points[:, :FIL], points[:, :FIL]], axis=1)
    rim_points = jnp.where(at_start, root_pair, rim_data[:, : 2 * FIL])
    extended = jnp.concatenate([rim_points, points], axis=1)
    node_count = points.shape[1]
    prev_one = extended[:, FIL : FIL + node_count]
    prev_two = extended[:, :node_count]
    first_prev = jnp.concatenate([rim_data[:, 2 * FIL :], first[:, :-FIL]], axis=1)
    is_root = at_start & (jnp.arange(node_count) < FIL)
    predicted = jnp.where(
        is_root[None, :], points, prev_one + AGE_STEP * 0.5 * (first_prev + first)
    )
    second = velocity(predicted)
    rim_second = passed_along(second[:, -FIL:], "band", 1)
    second_prev = jnp.concatenate([rim_second, second[:, :-FIL]], axis=1)
    updated = (
        prev_one
        + AGE_STEP * 0.25 * (first_prev + first + second_prev + second)
        - (points - 2.0 * prev_one + prev_two) / 6.0
    )
    updated = jnp.where(is_root[None, :], points, updated)
    return (updated[None], first[None])


def solution(mesh):
    placed = (
        P("row", None, "band"),
        P("row", None, "band"),
        P("row", "band"),
        P("row", None),
        P("row", None),
    )
    return jax.shard_map(
        local,
        mesh=mesh,
        in_specs=placed,
        out_specs=(P("row", None, "band"), P("row", None, "band")),
        check_vma=False,
    )
```

profile of v0, /device:TPU:29, one launch (start us, length us, event | category | flops | bytes accessed | tf_op | source)
XLA Modules:
  0.0 289.5 jit_solution(17327840383038286965)
XLA Ops:
  7.9 5.6 %all-gather = f32[1,3,512]{2,1,0:T(4,128)S(1)} all-gather(f32[1,3,128]{2,1,0:T(4,128)S(1)} %copy.38), channel_id=2, replica_groups=mesh['row'=8,'band'=4] {'band'}, dimensions={2}, use_global_device_ids=true | all-gather | bytes 7680 | tf_op jit(solution)/shard_map/all_gather | solution.py:73
  15.8 12.1 %while.86 = (s32[]{:T(128)}, f32[3,512]{1,0:T(4,128)S(1)}, f32[3,512]{1,0:T(4,128)S(1)}, f32[3,7,256]{2,1,0:T(8,128)S(1)}, s32[]{:T(128)}, /*index=5*/s32[]{:T(128)}, s32[]{}, s32[]{}) while((s32[]{:T(128)}, f32[3,512]{1,0:T(4,128)S(1)}, f32[3,512]{1,0:T(4,128)S(1)}, f32[3,7,256]{2,1,0:T(8,128)S(1)}, s32[]{:T(128)}, ...), condition=%wide.region_7.8_spmd.clone, body=%wide.region_0.7_spmd.clone.sunk | while | flops 5902853 | bytes 9489543 | solution.py:51
  15.9 1.6 multiply_reduce_fusion.16
  17.5 2.3 fusion.27
  19.9 1.6 multiply_reduce_fusion.16
  21.6 2.3 fusion.27
  23.9 1.6 multiply_reduce_fusion.16
  25.6 2.3 fusion.27
  28.0 83.9 %while.84 = (s32[]{:T(128)}, f32[7,768]{1,0:T(8,128)S(1)}, f32[3,512]{1,0:T(4,128)S(1)}, s32[]{:T(128)}, s32[3]{0:T(128)S(1)}, /*index=5*/pred[3]{0:T(512)(128)(4,1)S(1)}, f32[3,512]{1,0:T(4,128)S(1)}, s32[]{:T(128)}, s32[]{:T(128)}) while((s32[]{:T(128)}, f32[7,768]{1,0:T(8,128)S(1)}, f32[3,512]{1,0:T(4,128)S(1)}, s32[]{:T(128)}, ...), condition=%wide.region_20.21_spmd, body=%wide.region_8.20_spmd.sunk | while | flops 5904402 | bytes 9637285 | solution.py:86
  30.8 1.9 collective-permute-done.1
  35.3 1.9 collective-permute-done.1
  39.9 2.4 collective-permute-done.1
  45.0 14.9 %collective-permute-done.1 = f32[7,768]{1,0:T(8,128)S(1)} collective-permute-done((f32[7,768]{1,0:T(8,128)S(1)}, f32[7,768]{1,0:T(8,128)S(1)}, u32[]{:S(2)}, u32[]{:S(2)}) %collective-permute-start.1) | collective-permute-done | bytes 21536 | tf_op jit(solution)/shard_map/while/body/eval_jaxpr/ppermute | solution.py:18
  60.0 12.1 %conditional.4 = (f32[3,512]{1,0:T(4,128)S(1)}) conditional(s32[]{:T(128)} %convert_element_type.22, f32[3,512]{1,0:T(4,128)S(1)} %get-tuple-element.1035, (f32[7,768]{1,0:T(8,128)S(1)}, f32[3,512]{1,0:T(4,128)S(1)}, f32[3,512]{1,0:T(4,128)S(1)}) %tuple.213), branch_computations={%region_10.10_spmd, %region_11.19_spmd} | conditional | flops 5904389 | bytes 9508055 | solution.py:81
  60.0 12.1 %while.82 = (s32[]{:T(128)}, f32[3,512]{1,0:T(4,128)S(1)}, f32[3,512]{1,0:T(4,128)S(1)}, f32[3,7,256]{2,1,0:T(8,128)S(1)}, s32[]{:T(128)}, /*index=5*/s32[]{:T(128)}, s32[]{}, s32[]{}) while((s32[]{:T(128)}, f32[3,512]{1,0:T(4,128)S(1)}, f32[3,512]{1,0:T(4,128)S(1)}, f32[3,7,256]{2,1,0:T(8,128)S(1)}, s32[]{:T(128)}, ...), condition=%wide.region_19.18_spmd.clone, body=%wide.region_12.17_spmd.clone.sunk | while | flops 5902853 | bytes 9489543 | solution.py:51
  60.0 1.6 multiply_reduce_fusion.19
  61.6 2.3 fusion.30
  65.7 2.3 fusion.30
  69.7 2.3 fusion.30
  74.8 2.8 collective-permute-done.1
  77.6 12.1 %conditional.4 = (f32[3,512]{1,0:T(4,128)S(1)}) conditional(s32[]{:T(128)} %convert_element_type.22, f32[3,512]{1,0:T(4,128)S(1)} %get-tuple-element.1035, (f32[7,768]{1,0:T(8,128)S(1)}, f32[3,512]{1,0:T(4,128)S(1)}, f32[3,512]{1,0:T(4,128)S(1)}) %tuple.213), branch_computations={%region_10.10_spmd, %region_11.19_spmd} | conditional | flops 5904389 | bytes 9508055 | solution.py:81
  77.6 12.1 %while.82 = (s32[]{:T(128)}, f32[3,512]{1,0:T(4,128)S(1)}, f32[3,512]{1,0:T(4,128)S(1)}, f32[3,7,256]{2,1,0:T(8,128)S(1)}, s32[]{:T(128)}, /*index=5*/s32[]{:T(128)}, s32[]{}, s32[]{}) while((s32[]{:T(128)}, f32[3,512]{1,0:T(4,128)S(1)}, f32[3,512]{1,0:T(4,128)S(1)}, f32[3,7,256]{2,1,0:T(8,128)S(1)}, s32[]{:T(128)}, ...), condition=%wide.region_19.18_spmd.clone, body=%wide.region_12.17_spmd.clone.sunk | while | flops 5902853 | bytes 9489543 | solution.py:51
  79.2 2.3 fusion.30
  83.3 2.3 fusion.30
  87.3 2.3 fusion.30
  92.4 2.8 collective-permute-done.1
  95.2 12.1 %conditional.4 = (f32[3,512]{1,0:T(4,128)S(1)}) conditional(s32[]{:T(128)} %convert_element_type.22, f32[3,512]{1,0:T(4,128)S(1)} %get-tuple-element.1035, (f32[7,768]{1,0:T(8,128)S(1)}, f32[3,512]{1,0:T(4,128)S(1)}, f32[3,512]{1,0:T(4,128)S(1)}) %tuple.213), branch_computations={%region_10.10_spmd, %region_11.19_spmd} | conditional | flops 5904389 | bytes 9508055 | solution.py:81
  95.2 12.1 %while.82 = (s32[]{:T(128)}, f32[3,512]{1,0:T(4,128)S(1)}, f32[3,512]{1,0:T(4,128)S(1)}, f32[3,7,256]{2,1,0:T(8,128)S(1)}, s32[]{:T(128)}, /*index=5*/s32[]{:T(128)}, s32[]{}, s32[]{}) while((s32[]{:T(128)}, f32[3,512]{1,0:T(4,128)S(1)}, f32[3,512]{1,0:T(4,128)S(1)}, f32[3,7,256]{2,1,0:T(8,128)S(1)}, s32[]{:T(128)}, ...), condition=%wide.region_19.18_spmd.clone, body=%wide.region_12.17_spmd.clone.sunk | while | flops 5902853 | bytes 9489543 | solution.py:51
  96.9 2.3 fusion.30
  100.9 2.3 fusion.30
  104.9 2.3 fusion.30
  110.1 1.9 collective-permute-done.1
  112.9 28.2 %reduce-scatter.7.cloned.1.call-done = f32[128,3]{1,0:T(8,128)} async-done(((f32[512,3]{1,0:T(8,128)}), f32[128,3]{1,0:T(8,128)}) %reduce-scatter.7.cloned.1.call-update) | async-done | bytes 1552
  142.3 2.8 collective-permute-start.2
  146.0 5.6 %all_gather.7 = f32[3,512]{1,0:T(4,128)S(1)} all-gather(f32[3,128]{1,0:T(4,128)S(1)} %get-tuple-element.683), channel_id=1, replica_groups=mesh['row'=8,'band'=4] {'band'}, dimensions={1}, use_global_device_ids=true | all-gather | bytes 7680 | tf_op jit(solution)/shard_map/all_gather | solution.py:73
  151.7 12.1 %while.87 = (s32[]{:T(128)}, f32[3,512]{1,0:T(4,128)S(1)}, f32[3,512]{1,0:T(4,128)S(1)}, f32[3,7,256]{2,1,0:T(8,128)S(1)}, s32[]{:T(128)}, /*index=5*/s32[]{:T(128)}, s32[]{}, s32[]{}) while((s32[]{:T(128)}, f32[3,512]{1,0:T(4,128)S(1)}, f32[3,512]{1,0:T(4,128)S(1)}, f32[3,7,256]{2,1,0:T(8,128)S(1)}, s32[]{:T(128)}, ...), condition=%wide.region_29.30_spmd.clone, body=%wide.region_22.29_spmd.clone.sunk | while | flops 5902853 | bytes 9489543 | solution.py:51
  153.3 2.3 fusion.28
  157.4 2.3 fusion.28
  161.4 2.3 fusion.28
  163.8 83.9 %while.85 = (s32[]{:T(128)}, f32[7,768]{1,0:T(8,128)S(1)}, f32[3,512]{1,0:T(4,128)S(1)}, s32[]{:T(128)}, s32[3]{0:T(128)S(1)}, /*index=5*/pred[3]{0:T(512)(128)(4,1)S(1)}, f32[3,512]{1,0:T(4,128)S(1)}, s32[]{:T(128)}, s32[]{:T(128)}) while((s32[]{:T(128)}, f32[7,768]{1,0:T(8,128)S(1)}, f32[3,512]{1,0:T(4,128)S(1)}, s32[]{:T(128)}, ...), condition=%wide.region_42.43_spmd, body=%wide.region_30.42_spmd.sunk | while | flops 5904402 | bytes 9637285 | solution.py:86
  166.4 2.0 collective-permute-done
  170.9 2.0 collective-permute-done
  175.5 2.6 collective-permute-done
  180.7 15.0 %collective-permute-done = f32[7,768]{1,0:T(8,128)S(1)} collective-permute-done((f32[7,768]{1,0:T(8,128)S(1)}, f32[7,768]{1,0:T(8,128)S(1)}, u32[]{:S(2)}, u32[]{:S(2)}) %collective-permute-start) | collective-permute-done | bytes 21536 | tf_op jit(solution)/shard_map/while/body/eval_jaxpr/ppermute | solution.py:18
  195.7 12.1 %conditional.5 = (f32[3,512]{1,0:T(4,128)S(1)}) conditional(s32[]{:T(128)} %convert_element_type.23, f32[3,512]{1,0:T(4,128)S(1)} %get-tuple-element.1086, (f32[7,768]{1,0:T(8,128)S(1)}, f32[3,512]{1,0:T(4,128)S(1)}, f32[3,512]{1,0:T(4,128)S(1)}) %tuple.215), branch_computations={%region_32.32_spmd, %region_33.41_spmd} | conditional | flops 5904389 | bytes 9508055 | solution.py:81
  195.7 12.1 %while.83 = (s32[]{:T(128)}, f32[3,512]{1,0:T(4,128)S(1)}, f32[3,512]{1,0:T(4,128)S(1)}, f32[3,7,256]{2,1,0:T(8,128)S(1)}, s32[]{:T(128)}, /*index=5*/s32[]{:T(128)}, s32[]{}, s32[]{}) while((s32[]{:T(128)}, f32[3,512]{1,0:T(4,128)S(1)}, f32[3,512]{1,0:T(4,128)S(1)}, f32[3,7,256]{2,1,0:T(8,128)S(1)}, s32[]{:T(128)}, ...), condition=%wide.region_41.40_spmd.clone, body=%wide.region_34.39_spmd.clone.sunk | while | flops 5902853 | bytes 9489543 | solution.py:51
  197.4 2.3 fusion.29
  201.4 2.3 fusion.29
  205.4 2.3 fusion.29
  210.4 2.9 collective-permute-done
  213.3 12.1 %conditional.5 = (f32[3,512]{1,0:T(4,128)S(1)}) conditional(s32[]{:T(128)} %convert_element_type.23, f32[3,512]{1,0:T(4,128)S(1)} %get-tuple-element.1086, (f32[7,768]{1,0:T(8,128)S(1)}, f32[3,512]{1,0:T(4,128)S(1)}, f32[3,512]{1,0:T(4,128)S(1)}) %tuple.215), branch_computations={%region_32.32_spmd, %region_33.41_spmd} | conditional | flops 5904389 | bytes 9508055 | solution.py:81
  213.3 12.1 %while.83 = (s32[]{:T(128)}, f32[3,512]{1,0:T(4,128)S(1)}, f32[3,512]{1,0:T(4,128)S(1)}, f32[3,7,256]{2,1,0:T(8,128)S(1)}, s32[]{:T(128)}, /*index=5*/s32[]{:T(128)}, s32[]{}, s32[]{}) while((s32[]{:T(128)}, f32[3,512]{1,0:T(4,128)S(1)}, f32[3,512]{1,0:T(4,128)S(1)}, f32[3,7,256]{2,1,0:T(8,128)S(1)}, s32[]{:T(128)}, ...), condition=%wide.region_41.40_spmd.clone, body=%wide.region_34.39_spmd.clone.sunk | while | flops 5902853 | bytes 9489543 | solution.py:51
  215.0 2.3 fusion.29
  219.0 2.3 fusion.29
  223.1 2.3 fusion.29
  228.1 2.9 collective-permute-done
  230.9 12.1 %conditional.5 = (f32[3,512]{1,0:T(4,128)S(1)}) conditional(s32[]{:T(128)} %convert_element_type.23, f32[3,512]{1,0:T(4,128)S(1)} %get-tuple-element.1086, (f32[7,768]{1,0:T(8,128)S(1)}, f32[3,512]{1,0:T(4,128)S(1)}, f32[3,512]{1,0:T(4,128)S(1)}) %tuple.215), branch_computations={%region_32.32_spmd, %region_33.41_spmd} | conditional | flops 5904389 | bytes 9508055 | solution.py:81
  230.9 12.1 %while.83 = (s32[]{:T(128)}, f32[3,512]{1,0:T(4,128)S(1)}, f32[3,512]{1,0:T(4,128)S(1)}, f32[3,7,256]{2,1,0:T(8,128)S(1)}, s32[]{:T(128)}, /*index=5*/s32[]{:T(128)}, s32[]{}, s32[]{}) while((s32[]{:T(128)}, f32[3,512]{1,0:T(4,128)S(1)}, f32[3,512]{1,0:T(4,128)S(1)}, f32[3,7,256]{2,1,0:T(8,128)S(1)}, s32[]{:T(128)}, ...), condition=%wide.region_41.40_spmd.clone, body=%wide.region_34.39_spmd.clone.sunk | while | flops 5902853 | bytes 9489543 | solution.py:51
  232.6 2.3 fusion.29
  236.7 2.3 fusion.29
  240.7 2.3 fusion.29
  245.7 2.0 collective-permute-done
  248.5 28.8 %reduce-scatter.9.cloned.1.call-done = f32[128,3]{1,0:T(8,128)} async-done(((f32[512,3]{1,0:T(8,128)}), f32[128,3]{1,0:T(8,128)}) %reduce-scatter.9.cloned.1.call-update) | async-done | bytes 1552
  278.4 2.8 collective-permute-start.3
  (200 shorter events, 70.8 us)
Async XLA Ops:
  7.2 134.0 %reduce-scatter.7.cloned.1.call-start = ((), (), s32[]{:S(2)}) async-start(), calls=%async_computation.2 | async-start | bytes 327680
  15.8 12.2 %copy-start.1 = (f32[1,768]{1,0:T(1,128)S(1)}, f32[1,768]{1,0:T(1,128)}, u32[]{:S(2)}) copy-start(f32[1,768]{1,0:T(1,128)} %param.25) | copy-start | bytes 9220
  15.8 12.2 %copy-start.4 = (s32[1,3]{1,0:T(1,128)S(1)}, s32[1,3]{1,0:T(1,128)}, u32[]{:S(2)}) copy-start(s32[1,3]{1,0:T(1,128)} %param.27) | copy-start | bytes 40
  15.8 12.2 %copy-start = (s32[1,3]{1,0:T(1,128)S(1)}, s32[1,3]{1,0:T(1,128)}, u32[]{:S(2)}) copy-start(s32[1,3]{1,0:T(1,128)} %param.26) | copy-start | bytes 40
  28.0 114.0 %copy-start.2 = (f32[3]{0:T(128)S(1)}, f32[3]{0:T(128)}, u32[]{:S(2)}) copy-start(f32[3]{0:T(128)} %constant.140.clone) | copy-start | bytes 40
  28.0 117.9 %copy-start.3 = (f32[1,3,128]{2,0,1:T(1,128)S(1)}, f32[1,3,128]{2,0,1:T(1,128)}, u32[]{:S(2)}) copy-start(f32[1,3,128]{2,0,1:T(1,128)} %param.23) | copy-start | bytes 4612
  28.1 4.6 %collective-permute-start.1 = (f32[7,768]{1,0:T(8,128)S(1)}, f32[7,768]{1,0:T(8,128)S(1)}, u32[]{:S(2)}, u32[]{:S(2)}) collective-permute-start(f32[7,768]{1,0:T(8,128)S(1)} %get-tuple-element.1034), channel_id=1, source_target_pairs={{0,4},{4,8},{8,12},{12,16},{16,20},{20,24},{24,28},{1,5},{5,9},{9,... | collective-permute-start | bytes 64520 | tf_op jit(solution)/shard_map/while/body/eval_jaxpr/ppermute | solution.py:18
  32.6 4.6 %collective-permute-start.1 = (f32[7,768]{1,0:T(8,128)S(1)}, f32[7,768]{1,0:T(8,128)S(1)}, u32[]{:S(2)}, u32[]{:S(2)}) collective-permute-start(f32[7,768]{1,0:T(8,128)S(1)} %get-tuple-element.1034), channel_id=1, source_target_pairs={{0,4},{4,8},{8,12},{12,16},{16,20},{20,24},{24,28},{1,5},{5,9},{9,... | collective-permute-start | bytes 64520 | tf_op jit(solution)/shard_map/while/body/eval_jaxpr/ppermute | solution.py:18
  37.2 5.1 %collective-permute-start.1 = (f32[7,768]{1,0:T(8,128)S(1)}, f32[7,768]{1,0:T(8,128)S(1)}, u32[]{:S(2)}, u32[]{:S(2)}) collective-permute-start(f32[7,768]{1,0:T(8,128)S(1)} %get-tuple-element.1034), channel_id=1, source_target_pairs={{0,4},{4,8},{8,12},{12,16},{16,20},{20,24},{24,28},{1,5},{5,9},{9,... | collective-permute-start | bytes 64520 | tf_op jit(solution)/shard_map/while/body/eval_jaxpr/ppermute | solution.py:18
  42.3 17.6 %collective-permute-start.1 = (f32[7,768]{1,0:T(8,128)S(1)}, f32[7,768]{1,0:T(8,128)S(1)}, u32[]{:S(2)}, u32[]{:S(2)}) collective-permute-start(f32[7,768]{1,0:T(8,128)S(1)} %get-tuple-element.1034), channel_id=1, source_target_pairs={{0,4},{4,8},{8,12},{12,16},{16,20},{20,24},{24,28},{1,5},{5,9},{9,... | collective-permute-start | bytes 64520 | tf_op jit(solution)/shard_map/while/body/eval_jaxpr/ppermute | solution.py:18
  72.1 5.5 %collective-permute-start.1 = (f32[7,768]{1,0:T(8,128)S(1)}, f32[7,768]{1,0:T(8,128)S(1)}, u32[]{:S(2)}, u32[]{:S(2)}) collective-permute-start(f32[7,768]{1,0:T(8,128)S(1)} %get-tuple-element.1034), channel_id=1, source_target_pairs={{0,4},{4,8},{8,12},{12,16},{16,20},{20,24},{24,28},{1,5},{5,9},{9,... | collective-permute-start | bytes 64520 | tf_op jit(solution)/shard_map/while/body/eval_jaxpr/ppermute | solution.py:18
  89.7 5.5 %collective-permute-start.1 = (f32[7,768]{1,0:T(8,128)S(1)}, f32[7,768]{1,0:T(8,128)S(1)}, u32[]{:S(2)}, u32[]{:S(2)}) collective-permute-start(f32[7,768]{1,0:T(8,128)S(1)} %get-tuple-element.1034), channel_id=1, source_target_pairs={{0,4},{4,8},{8,12},{12,16},{16,20},{20,24},{24,28},{1,5},{5,9},{9,... | collective-permute-start | bytes 64520 | tf_op jit(solution)/shard_map/while/body/eval_jaxpr/ppermute | solution.py:18
  107.3 4.6 %collective-permute-start.1 = (f32[7,768]{1,0:T(8,128)S(1)}, f32[7,768]{1,0:T(8,128)S(1)}, u32[]{:S(2)}, u32[]{:S(2)}) collective-permute-start(f32[7,768]{1,0:T(8,128)S(1)} %get-tuple-element.1034), channel_id=1, source_target_pairs={{0,4},{4,8},{8,12},{12,16},{16,20},{20,24},{24,28},{1,5},{5,9},{9,... | collective-permute-start | bytes 64520 | tf_op jit(solution)/shard_map/while/body/eval_jaxpr/ppermute | solution.py:18
  112.8 164.6 %reduce-scatter.9.cloned.1.call-start = ((), (), s32[]{:S(2)}) async-start(), calls=%async_computation.3 | async-start | bytes 327680
  142.3 3.5 %collective-permute-start.2 = (f32[3,24]{1,0:T(4,128)S(1)}, f32[3,24]{1,0:T(4,128)S(1)}, u32[]{:S(2)}, u32[]{:S(2)}) collective-permute-start(f32[3,24]{1,0:T(4,128)S(1)} %pad_maximum_fusion.2), channel_id=1, source_target_pairs={{0,1},{1,2},{2,3},{4,5},{5,6},{6,7},{8,9},{9,10},{10,11},{12,13},{... | collective-permute-start | bytes 872 | tf_op jit(solution)/shard_map/ppermute | solution.py:18
  163.8 4.6 %collective-permute-start = (f32[7,768]{1,0:T(8,128)S(1)}, f32[7,768]{1,0:T(8,128)S(1)}, u32[]{:S(2)}, u32[]{:S(2)}) collective-permute-start(f32[7,768]{1,0:T(8,128)S(1)} %get-tuple-element.1085), channel_id=1, source_target_pairs={{0,4},{4,8},{8,12},{12,16},{16,20},{20,24},{24,28},{1,5},{5,9},{9,... | collective-permute-start | bytes 64520 | tf_op jit(solution)/shard_map/while/body/eval_jaxpr/ppermute | solution.py:18
  168.4 4.6 %collective-permute-start = (f32[7,768]{1,0:T(8,128)S(1)}, f32[7,768]{1,0:T(8,128)S(1)}, u32[]{:S(2)}, u32[]{:S(2)}) collective-permute-start(f32[7,768]{1,0:T(8,128)S(1)} %get-tuple-element.1085), channel_id=1, source_target_pairs={{0,4},{4,8},{8,12},{12,16},{16,20},{20,24},{24,28},{1,5},{5,9},{9,... | collective-permute-start | bytes 64520 | tf_op jit(solution)/shard_map/while/body/eval_jaxpr/ppermute | solution.py:18
  172.9 5.2 %collective-permute-start = (f32[7,768]{1,0:T(8,128)S(1)}, f32[7,768]{1,0:T(8,128)S(1)}, u32[]{:S(2)}, u32[]{:S(2)}) collective-permute-start(f32[7,768]{1,0:T(8,128)S(1)} %get-tuple-element.1085), channel_id=1, source_target_pairs={{0,4},{4,8},{8,12},{12,16},{16,20},{20,24},{24,28},{1,5},{5,9},{9,... | collective-permute-start | bytes 64520 | tf_op jit(solution)/shard_map/while/body/eval_jaxpr/ppermute | solution.py:18
  178.1 17.6 %collective-permute-start = (f32[7,768]{1,0:T(8,128)S(1)}, f32[7,768]{1,0:T(8,128)S(1)}, u32[]{:S(2)}, u32[]{:S(2)}) collective-permute-start(f32[7,768]{1,0:T(8,128)S(1)} %get-tuple-element.1085), channel_id=1, source_target_pairs={{0,4},{4,8},{8,12},{12,16},{16,20},{20,24},{24,28},{1,5},{5,9},{9,... | collective-permute-start | bytes 64520 | tf_op jit(solution)/shard_map/while/body/eval_jaxpr/ppermute | solution.py:18
  207.8 5.5 %collective-permute-start = (f32[7,768]{1,0:T(8,128)S(1)}, f32[7,768]{1,0:T(8,128)S(1)}, u32[]{:S(2)}, u32[]{:S(2)}) collective-permute-start(f32[7,768]{1,0:T(8,128)S(1)} %get-tuple-element.1085), channel_id=1, source_target_pairs={{0,4},{4,8},{8,12},{12,16},{16,20},{20,24},{24,28},{1,5},{5,9},{9,... | collective-permute-start | bytes 64520 | tf_op jit(solution)/shard_map/while/body/eval_jaxpr/ppermute | solution.py:18
  225.5 5.5 %collective-permute-start = (f32[7,768]{1,0:T(8,128)S(1)}, f32[7,768]{1,0:T(8,128)S(1)}, u32[]{:S(2)}, u32[]{:S(2)}) collective-permute-start(f32[7,768]{1,0:T(8,128)S(1)} %get-tuple-element.1085), channel_id=1, source_target_pairs={{0,4},{4,8},{8,12},{12,16},{16,20},{20,24},{24,28},{1,5},{5,9},{9,... | collective-permute-start | bytes 64520 | tf_op jit(solution)/shard_map/while/body/eval_jaxpr/ppermute | solution.py:18
  243.1 4.6 %collective-permute-start = (f32[7,768]{1,0:T(8,128)S(1)}, f32[7,768]{1,0:T(8,128)S(1)}, u32[]{:S(2)}, u32[]{:S(2)}) collective-permute-start(f32[7,768]{1,0:T(8,128)S(1)} %get-tuple-element.1085), channel_id=1, source_target_pairs={{0,4},{4,8},{8,12},{12,16},{16,20},{20,24},{24,28},{1,5},{5,9},{9,... | collective-permute-start | bytes 64520 | tf_op jit(solution)/shard_map/while/body/eval_jaxpr/ppermute | solution.py:18
  278.4 3.5 %collective-permute-start.3 = (f32[3,8]{1,0:T(4,128)S(1)}, f32[3,8]{1,0:T(4,128)S(1)}, u32[]{:S(2)}, u32[]{:S(2)}) collective-permute-start(f32[3,8]{1,0:T(4,128)S(1)} %slice.182), channel_id=1, source_target_pairs={{0,1},{1,2},{2,3},{4,5},{5,6},{6,7},{8,9},{9,10},{10,11},{12,13},{... | collective-permute-start | bytes 296 | tf_op jit(solution)/shard_map/ppermute | solution.py:18
Sparse Core Ops, SparseCore 0:
  112.9 28.2 reduce-scatter.6
  248.7 28.6 reduce-scatter.8
where the time goes:
time: 288 us; the launch traced here: 289 us
  waiting for transfers between devices  116 us (40%)
  other arithmetic  107 us (37%)
  starting transfers between devices  23.7 us (8%)
  between operations  14.2 us (5%)
  blocking collectives  11.2 us (4%)
  loops' own time  10.5 us (4%)
  local copies, waits for them, and re-layouts  6.82 us (2%)
    ppermute x16, waiting for transfers between devices, passed_along(): return lax.ppermute(block, axis, route)  58.6 us
    unnamed x4, waiting for transfers between devices  57.1 us
    reduce_sum x24, other arithmetic, segment_piece(): jnp.sum(cross_x * factor, axis=1)  55.7 us
    reduce_sum x24, other arithmetic, segment_piece(): norm_one = jnp.sqrt(jnp.sum(rel_one * rel_one, axis=0) + CORE_SQUARE)  39.6 us
    ppermute x16, starting transfers between devices, passed_along(): return lax.ppermute(block, axis, route)  23.6 us
    all_gather x2, blocking collectives, velocity(): targets = lax.all_gather(where_at, 'band', axis=1, tiled=True)  11.2 us
    another operation x2, loops' own time, velocity(): ignored, total = lax.fori_loop(0, reach, one_hop, (own_block, total))  9.83 us
    reduce_or x14, other arithmetic, one_hop(): matched = jnp.any((listed == source) & active)  9.46 us
  transfers between devices with their start and end apart: 18, of which 18 were waited for; matrix products, arithmetic and copies ran while one was open for 3% of the time, Pallas kernels for 0%

commit v1 on v0

v1 whole, which is shorter than its diff:
```python
import functools
import math

import jax
import jax.numpy as jnp
from jax import lax
from jax.experimental import pallas as pl
from jax.experimental.pallas import tpu as pltpu
from jax.sharding import PartitionSpec as P

FIL = 8
CORE_SQUARE = 0.04
AGE_STEP = 0.25
LISTED = 3
TILE = 256
F32, BF16 = jnp.float32, jnp.bfloat16


def split(value):
    high = value.astype(BF16).astype(F32)
    rest = value - high
    middle = rest.astype(BF16).astype(F32)
    return high, middle, rest - middle


def point_factors(points, norms_row):
    count = points.shape[1]
    zeros = lambda rows: jnp.zeros((rows, count), F32)
    terms = split(-2.0 * points)
    squared = jnp.sum(points * points, axis=0, keepdims=True)
    rows = []
    for term in (0, 1, 2, 0, 1, 2, 0, 1):
        rows += [zeros(3), terms[term], zeros(2)] if norms_row else [terms[term], zeros(5)]
    one = jnp.ones((1, count), F32)
    for _ in range(3):
        rows += [zeros(1), one, zeros(6)] if norms_row else [one, zeros(7)]
    rows += [*split(squared), zeros(5)]
    return jnp.concatenate(rows, axis=0).T.astype(BF16)


def segment_factors(block):
    one = jnp.ones((1, block.shape[1]), F32)
    zero = jnp.zeros_like(one)
    start = [block[i : i + 1] for i in range(3)]
    end = [block[i : i + 1] for i in range(3, 6)]
    scale = block[6:7] * (0.5 / math.pi)
    along = [a - b for a, b in zip(start, end)]
    moment = [
        start[1] * end[2] - start[2] * end[1],
        start[2] * end[0] - start[0] * end[2],
        start[0] * end[1] - start[1] * end[0],
    ]
    square = lambda v: v[0] * v[0] + v[1] * v[1] + v[2] * v[2]
    norms = jnp.concatenate(
        [square(start) + CORE_SQUARE, square(end) + CORE_SQUARE] + [zero] * 6, axis=0
    )
    high, middle, low = split(block)
    constant = jnp.concatenate([one] * 3 + [zero] * 5, axis=0)
    distance = jnp.concatenate(
        [high, high, high, middle, middle, middle, low, low, *split(norms), constant], axis=0
    ).astype(BF16)
    weights = jnp.concatenate([scale * v for v in along + moment] + [zero] * 2, axis=0)
    cross = jnp.concatenate([*split(weights), jnp.zeros_like(weights)], axis=0).astype(BF16)
    return distance, cross, square(along) + 2.0 * CORE_SQUARE


def kernel(
    bands, group, upstream, mask, here, there, updated_ref, first_ref, distance, cross, length
):
    own = group
    seg_count = here.shape[2]
    wake_slots = group + 1
    row, band = lax.axis_index("row"), lax.axis_index("band")
    count = updated_ref.shape[2]
    total_points = count + 2 * FIL
    used = mask[0, 0] + mask[0, 1] + mask[0, 2]

    def part_ref(part):
        half = bands // 2
        return (here, part) if part < half else (there, part - half)

    def slot_of(wake):
        listed = jnp.where(wake == 1, upstream[0, 0], jnp.where(wake == 2, upstream[0, 1], upstream[0, 2]))
        position = lax.rem(listed, group) ^ lax.rem(row, group)
        return jnp.where(wake == 0, own, position)

    def block_of(part, slot):
        ref, at = part_ref(part)
        return ref[at * wake_slots + slot]

    def node_block(block):
        return jnp.concatenate(
            [block[7:8, i * count : (i + 1) * count] for i in range(3)], axis=0
        )

    points = node_block(here[own])
    before = jnp.zeros_like(points)
    for part in range(1, bands):
        flip = sum(bands >> (bit + 1) for bit in range(bands.bit_length()) if part >> bit & 1)
        before = jnp.where(band ^ flip == band - 1, node_block(block_of(part, own)), before)
    at_start = band == 0
    root = points[:, :FIL]
    halo = jnp.where(at_start, jnp.concatenate([root, root], axis=1), before[:, -2 * FIL :])
    extended = jnp.concatenate([halo, points], axis=1)

    def add_tile(factors, total, wake, offset):
        at = pl.ds(offset, TILE)
        squared = jnp.dot(factors, distance[wake, :, at], preferred_element_type=F32)
        squared_one, squared_two = squared[:total_points], squared[total_points:]
        inverse_one, inverse_two = lax.rsqrt(squared_one), lax.rsqrt(squared_two)
        norms = squared_one * inverse_one + squared_two * inverse_two
        factor = (inverse_one + inverse_two) * pltpu.reciprocal(
            norms * norms - length[wake, :, at], approx=True
        )
        high = factor.astype(BF16)
        low = (factor - high.astype(F32)).astype(BF16)
        weights = cross[wake, :, at]
        contract = (((1,), (1,)), ((), ()))
        return (
            total
            + lax.dot_general(weights, high, contract, preferred_element_type=F32)
            + lax.dot_general(weights, low, contract, preferred_element_type=F32)
        )

    def velocity(where_at, prepare):
        factors = jnp.concatenate(
            [point_factors(where_at, 0), point_factors(where_at, 1)], axis=0
        )

        def one_wake(wake, total):
            if prepare:
                slot = slot_of(wake)
                for part in range(bands):
                    at = pl.ds(part * seg_count, seg_count)
                    parts = segment_factors(block_of(part, slot))
                    distance[wake, :, at], cross[wake, :, at], length[wake, :, at] = parts
            for tile in range(bands * seg_count // TILE):
                total = add_tile(factors, total, wake, tile * TILE)
            return total

        total = lax.fori_loop(0, 1 + used, one_wake, jnp.zeros((32, total_points), F32))
        sums = total[0:8] + total[8:16] + total[16:24]
        x, y, z = where_at[0:1], where_at[1:2], where_at[2:3]
        dx, dy, dz = sums[0:1], sums[1:2], sums[2:3]
        return jnp.concatenate(
            [
                y * dz - z * dy + sums[3:4] + 1.0,
                z * dx - x * dz + sums[4:5],
                x * dy - y * dx + sums[5:6],
            ],
            axis=0,
        )

    def shifted(field):
        return jnp.concatenate([field[:, :FIL], field[:, :-FIL]], axis=1)

    lane = lax.broadcasted_iota(jnp.int32, (3, total_points), 1)
    first = velocity(extended, True)
    pair = first + shifted(first)
    previous = shifted(extended)
    kept = (lane < FIL) | (at_start & (lane >= 2 * FIL) & (lane < 3 * FIL))
    predicted = jnp.where(kept, extended, previous + AGE_STEP * 0.5 * pair)
    second = velocity(predicted, False)
    pair = pair + second + shifted(second)
    updated = (
        previous + AGE_STEP * 0.25 * pair - (extended - 2.0 * previous + shifted(previous)) / 6.0
    )
    updated = jnp.where(kept, extended, updated)
    updated_ref[0] = updated[:, 2 * FIL :]
    first_ref[0] = first[:, 2 * FIL :]


def local(nodes, segments, circulation, upstream, upstream_mask):
    rows, bands = lax.axis_size("row"), lax.axis_size("band")
    group = min(8, rows // 2)
    seg_count = segments.shape[2]
    count = nodes.shape[2]
    node_row = jnp.pad(nodes.reshape(1, 3 * count), ((0, 0), (0, seg_count - 3 * count)))
    own = jnp.concatenate([segments[0], circulation, node_row], axis=0)[None]

    wakes, bit = own, 1
    while bit < group // 2:
        route = [(i, i ^ bit) for i in range(rows - group)]
        wakes = jnp.concatenate([wakes, lax.ppermute(wakes, "row", route)])
        bit *= 2
    arrived = [
        lax.ppermute(wakes, "row", [(i, (i ^ flip) + group) for i in range(rows - group)])
        for flip in ((0, bit) if group > 1 else (0,))
    ]
    here = jnp.concatenate(arrived + [own])
    bit = bands // 2
    while bit > 1:
        route = [(i, i ^ bit) for i in range(bands)]
        here = jnp.concatenate([here, lax.ppermute(here, "band", route)])
        bit //= 2
    there = lax.ppermute(here, "band", [(i, i ^ 1) for i in range(bands)])

    whole = pl.BlockSpec(memory_space=pltpu.VMEM)
    scalars = pl.BlockSpec(memory_space=pltpu.SMEM)
    out = jax.ShapeDtypeStruct((1, 3, count), F32)
    segs = bands * seg_count
    return pl.pallas_call(
        functools.partial(kernel, bands, group),
        out_shape=(out, out),
        in_specs=[scalars, scalars, whole, whole],
        out_specs=(whole, whole),
        scratch_shapes=[
            pltpu.VMEM((1 + LISTED, 96, segs), BF16),
            pltpu.VMEM((1 + LISTED, 32, segs), BF16),
            pltpu.VMEM((1 + LISTED, 1, segs), F32),
        ],
        compiler_params=pltpu.CompilerParams(vmem_limit_bytes=32 * 2**20),
    )(upstream, upstream_mask, here, there)


def solution(mesh):
    placed = (
        P("row", None, "band"),
        P("row", None, "band"),
        P("row", "band"),
        P("row", None),
        P("row", None),
    )
    return jax.shard_map(
        local,
        mesh=mesh,
        in_specs=placed,
        out_specs=(P("row", None, "band"), P("row", None, "band")),
        check_vma=False,
    )
```

time: 288 us -> 33.3 us (0.12)
  other arithmetic: 107 us -> 0.05 us
  waiting for transfers between devices: 116 us -> 10.5 us
  starting transfers between devices: 23.7 us -> 7.58 us
  between operations: 14.2 us -> 0.71 us
  Pallas kernels: 0 us -> 11.6 us
  blocking collectives: 11.2 us -> 0 us
  loops' own time: 10.5 us -> 0 us
  local copies, waits for them, and re-layouts: 6.82 us -> 2.56 us
    reduce_sum x48 -> x0, other arithmetic: 95.3 us -> none  [the longest x24 55.7 us: segment_piece(): jnp.sum(cross_x * factor, axis=1)]
    unnamed x4 -> x0, waiting for transfers between devices: 57.1 us -> none
    ppermute x16 -> x5, waiting for transfers between devices: 58.6 us -> 10.5 us  [the longest x2 6.81 us: local(): lax.ppermute(wakes, 'row', [(i, (i ^ flip) + group) for i in range(rows -...]
    ppermute x16 -> x5, starting transfers between devices: 23.6 us -> 7.58 us  [the longest x1 3.06 us: local(): there = lax.ppermute(here, 'band', [(i, i ^ 1) for i in range(bands)])]
    pallas_call x0 -> x1, Pallas kernels: none -> 11.6 us  [local(): pl.pallas_call(functools.partial(kernel, bands, group), out_shape=(out, o...]
    all_gather x2 -> x0, blocking collectives: 11.2 us -> none  [velocity(): targets = lax.all_gather(where_at, 'band', axis=1, tiled=True)]
    another operation x24 -> x0, loops' own time: 10.5 us -> none  [the longest x2 9.83 us: velocity(): ignored, total = lax.fori_loop(0, reach, one_hop, (own_block, total))]
    reduce_or x14 -> x0, other arithmetic: 9.46 us -> none  [one_hop(): matched = jnp.any((listed == source) & active)]
  transfers between devices with their start and end apart: 18 -> 5, of which waited for: 18 -> 4; matrix products, arithmetic and copies ran while one was open for 3% -> 0% of each run, Pallas kernels for 0% -> 0%
where the time goes in v1:
time: 33.3 us; the launch traced here: 33 us
  Pallas kernels  11.6 us (35%)
  waiting for transfers between devices  10.5 us (32%)
  starting transfers between devices  7.58 us (23%)
  local copies, waits for them, and re-layouts  2.56 us (8%)
  between operations  0.71 us (2%)
    pallas_call x1, Pallas kernels, local(): pl.pallas_call(functools.partial(kernel, bands, group), out_shape=(out, o...  11.6 us
    ppermute x2, waiting for transfers between devices, local(): lax.ppermute(wakes, 'row', [(i, (i ^ flip) + group) for i in range(rows -...  6.81 us
    ppermute x1, starting transfers between devices, local(): there = lax.ppermute(here, 'band', [(i, i ^ 1) for i in range(bands)])  3.06 us
    ppermute x2, starting transfers between devices, local(): lax.ppermute(wakes, 'row', [(i, (i ^ flip) + group) for i in range(rows -...  2.58 us
    ppermute x1, waiting for transfers between devices, local(): here = jnp.concatenate([here, lax.ppermute(here, 'band', route)])  2.52 us
    unnamed x9, local copies, waits for them, and re-layouts  1.43 us
    ppermute x1, starting transfers between devices, local(): here = jnp.concatenate([here, lax.ppermute(here, 'band', route)])  1.28 us
    ppermute x1, waiting for transfers between devices, local(): there = lax.ppermute(here, 'band', [(i, i ^ 1) for i in range(bands)])  1.14 us
  transfers between devices with their start and end apart: 5, of which 4 were waited for; matrix products, arithmetic and copies ran while one was open for 0% of the time, Pallas kernels for 0%

profile of v1, /device:TPU:29, one launch (start us, length us, event | category | flops | bytes accessed | tf_op | source)
XLA Modules:
  0.0 33.0 jit_solution(9513377977015571763)
XLA Ops:
  0.6 0.0 copy-start.3
  0.6 0.7 %copy.11 = f32[1,6,768]{2,1,0:T(8,128)S(1)} copy(f32[1,6,768]{2,0,1:T(1,128)} %param.6) | data formatting | bytes 36864
  1.4 0.0 copy-start.2
  1.4 0.0 copy-done.3
  1.4 0.7 %copy-done.2 = f32[1,768]{1,0:T(1,128)S(1)} copy-done((f32[1,768]{1,0:T(1,128)S(1)}, f32[1,768]{1,0:T(1,128)}, u32[]{:S(2)}) %copy-start.2) | copy-done | bytes 3096
  2.1 0.7 %collective-permute-start = (f32[1,8,768]{2,1,0:T(8,128)S(1)}, f32[1,8,768]{2,1,0:T(8,128)S(1)}, u32[]{:S(2)}, u32[]{:S(2)}) collective-permute-start(f32[1,8,768]{2,1,0:T(8,128)S(1)} %fusion), channel_id=1, source_target_pairs={{0,4},{4,0},{8,12},{12,8},{1,5},{5,1},{9,13},{13,9},{2,6},{6,2},{1... | collective-permute-start | bytes 73736 | tf_op jit(solution)/shard_map/ppermute | solution.py:184
  2.7 0.0 collective-permute-done
  2.8 1.3 %collective-permute-start.2 = (f32[2,8,768]{2,1,0:T(8,128)S(1)}, f32[2,8,768]{2,1,0:T(8,128)S(1)}, u32[]{:S(2)}, u32[]{:S(2)}) collective-permute-start(f32[2,8,768]{2,1,0:T(8,128)S(1)} %pad_maximum_fusion.2), channel_id=1, source_target_pairs={{0,24},{4,28},{8,16},{12,20},{1,25},{5,29},{9,17},{13,21},{2,26},{... | collective-permute-start | bytes 147464 | tf_op jit(solution)/shard_map/ppermute | solution.py:187
  4.1 1.3 %collective-permute-start.1 = (f32[2,8,768]{2,1,0:T(8,128)S(1)}, f32[2,8,768]{2,1,0:T(8,128)S(1)}, u32[]{:S(2)}, u32[]{:S(2)}) collective-permute-start(f32[2,8,768]{2,1,0:T(8,128)S(1)} %pad_maximum_fusion.2), channel_id=1, source_target_pairs={{0,16},{4,20},{8,24},{12,28},{1,17},{5,21},{9,25},{13,29},{2,18},{... | collective-permute-start | bytes 147464 | tf_op jit(solution)/shard_map/ppermute | solution.py:187
  5.4 4.1 %collective-permute-done.2 = f32[2,8,768]{2,1,0:T(8,128)S(1)} collective-permute-done((f32[2,8,768]{2,1,0:T(8,128)S(1)}, f32[2,8,768]{2,1,0:T(8,128)S(1)}, u32[]{:S(2)}, u32[]{:S(2)}) %collective-permute-start.2) | collective-permute-done | bytes 49184 | tf_op jit(solution)/shard_map/ppermute | solution.py:187
  9.4 2.7 %collective-permute-done.1 = f32[2,8,768]{2,1,0:T(8,128)S(1)} collective-permute-done((f32[2,8,768]{2,1,0:T(8,128)S(1)}, f32[2,8,768]{2,1,0:T(8,128)S(1)}, u32[]{:S(2)}, u32[]{:S(2)}) %collective-permute-start.1) | collective-permute-done | bytes 49184 | tf_op jit(solution)/shard_map/ppermute | solution.py:187
  12.2 0.0 copy-start
  12.2 0.0 copy-start.1
  12.2 1.3 %collective-permute-start.3 = (f32[5,8,768]{2,1,0:T(8,128)S(1)}, f32[5,8,768]{2,1,0:T(8,128)S(1)}, u32[]{:S(2)}, u32[]{:S(2)}) collective-permute-start(f32[5,8,768]{2,1,0:T(8,128)S(1)} %pad_maximum_fusion.1), channel_id=1, source_target_pairs={{0,2},{1,3},{2,0},{3,1},{4,6},{5,7},{6,4},{7,5},{8,10},{9,11},{10,... | collective-permute-start | bytes 368648 | tf_op jit(solution)/shard_map/ppermute | solution.py:194
  13.5 2.5 %collective-permute-done.3 = f32[5,8,768]{2,1,0:T(8,128)S(1)} collective-permute-done((f32[5,8,768]{2,1,0:T(8,128)S(1)}, f32[5,8,768]{2,1,0:T(8,128)S(1)}, u32[]{:S(2)}, u32[]{:S(2)}) %collective-permute-start.3) | collective-permute-done | bytes 122912 | tf_op jit(solution)/shard_map/ppermute | solution.py:194
  16.0 3.1 %collective-permute-start.4 = (f32[10,8,768]{2,1,0:T(8,128)S(1)}, f32[10,8,768]{2,1,0:T(8,128)S(1)}, u32[]{:S(2)}, u32[]{:S(2)}) collective-permute-start(f32[10,8,768]{2,1,0:T(8,128)S(1)} %pad_maximum_fusion.here), channel_id=1, source_target_pairs={{0,1},{1,0},{2,3},{3,2},{4,5},{5,4},{6,7},{7,6},{8,9},{9,8},{10,11... | collective-permute-start | bytes 737288 | tf_op jit(solution)/shard_map/ppermute | solution.py:196
  19.1 1.1 %collective-permute-done.4.there = f32[10,8,768]{2,1,0:T(8,128)S(1)} collective-permute-done((f32[10,8,768]{2,1,0:T(8,128)S(1)}, f32[10,8,768]{2,1,0:T(8,128)S(1)}, u32[]{:S(2)}, u32[]{:S(2)}) %collective-permute-start.4) | collective-permute-done | bytes 245792 | tf_op jit(solution)/shard_map/ppermute | solution.py:196
  20.2 0.0 copy-done
  20.2 0.0 copy-done.1
  20.2 11.6 %shard_map.68 = (f32[1,3,128]{2,1,0:T(4,128)S(1)}, f32[1,3,128]{2,1,0:T(4,128)S(1)}) custom-call(s32[1,3]{1,0:T(1,128)S(1)} %copy-done, s32[1,3]{1,0:T(1,128)S(1)} %copy-done.1, f32[10,8,768]{2,1,0:T(8,128)S(1)} %pad_maximum_fusion.here, f32[10,8,768]{2,1,0:T(8,128)S(1)} %collective-permute-done.4.there), custom_call_target="tpu_custom_call" | custom-call | tf_op jit(solution)/shard_map/pallas_call | solution.py:202
  31.9 0.6 %copy.7 = f32[1,3,128]{2,0,1:T(1,128)} copy(f32[1,3,128]{2,1,0:T(4,128)S(1)} %get-tuple-element.2) | data formatting | bytes 3072 | tf_op jit(solution)/shard_map/pallas_call | solution.py:202
  32.4 0.6 %copy.8 = f32[1,3,128]{2,0,1:T(1,128)} copy(f32[1,3,128]{2,1,0:T(4,128)S(1)} %get-tuple-element.3) | data formatting | bytes 3072 | tf_op jit(solution)/shard_map/pallas_call | solution.py:202
  (4 shorter events, 0.0 us)
Async XLA Ops:
  0.6 0.7 %copy-start.3 = (f32[1,3,128]{2,0,1:T(1,128)S(1)}, f32[1,3,128]{2,0,1:T(1,128)}, u32[]{:S(2)}) copy-start(f32[1,3,128]{2,0,1:T(1,128)} %param.5) | copy-start | bytes 4612
  1.4 0.7 %copy-start.2 = (f32[1,768]{1,0:T(1,128)S(1)}, f32[1,768]{1,0:T(1,128)}, u32[]{:S(2)}) copy-start(f32[1,768]{1,0:T(1,128)} %param.7) | copy-start | bytes 9220
  2.1 0.7 %collective-permute-start = (f32[1,8,768]{2,1,0:T(8,128)S(1)}, f32[1,8,768]{2,1,0:T(8,128)S(1)}, u32[]{:S(2)}, u32[]{:S(2)}) collective-permute-start(f32[1,8,768]{2,1,0:T(8,128)S(1)} %fusion), channel_id=1, source_target_pairs={{0,4},{4,0},{8,12},{12,8},{1,5},{5,1},{9,13},{13,9},{2,6},{6,2},{1... | collective-permute-start | bytes 73736 | tf_op jit(solution)/shard_map/ppermute | solution.py:184
  2.8 6.7 %collective-permute-start.2 = (f32[2,8,768]{2,1,0:T(8,128)S(1)}, f32[2,8,768]{2,1,0:T(8,128)S(1)}, u32[]{:S(2)}, u32[]{:S(2)}) collective-permute-start(f32[2,8,768]{2,1,0:T(8,128)S(1)} %pad_maximum_fusion.2), channel_id=1, source_target_pairs={{0,24},{4,28},{8,16},{12,20},{1,25},{5,29},{9,17},{13,21},{2,26},{... | collective-permute-start | bytes 147464 | tf_op jit(solution)/shard_map/ppermute | solution.py:187
  4.1 8.1 %collective-permute-start.1 = (f32[2,8,768]{2,1,0:T(8,128)S(1)}, f32[2,8,768]{2,1,0:T(8,128)S(1)}, u32[]{:S(2)}, u32[]{:S(2)}) collective-permute-start(f32[2,8,768]{2,1,0:T(8,128)S(1)} %pad_maximum_fusion.2), channel_id=1, source_target_pairs={{0,16},{4,20},{8,24},{12,28},{1,17},{5,21},{9,25},{13,29},{2,18},{... | collective-permute-start | bytes 147464 | tf_op jit(solution)/shard_map/ppermute | solution.py:187
  12.2 8.0 %copy-start = (s32[1,3]{1,0:T(1,128)S(1)}, s32[1,3]{1,0:T(1,128)}, u32[]{:S(2)}) copy-start(s32[1,3]{1,0:T(1,128)} %upstream.1) | copy-start | bytes 40
  12.2 8.0 %copy-start.1 = (s32[1,3]{1,0:T(1,128)S(1)}, s32[1,3]{1,0:T(1,128)}, u32[]{:S(2)}) copy-start(s32[1,3]{1,0:T(1,128)} %mask.1) | copy-start | bytes 40
  12.2 3.8 %collective-permute-start.3 = (f32[5,8,768]{2,1,0:T(8,128)S(1)}, f32[5,8,768]{2,1,0:T(8,128)S(1)}, u32[]{:S(2)}, u32[]{:S(2)}) collective-permute-start(f32[5,8,768]{2,1,0:T(8,128)S(1)} %pad_maximum_fusion.1), channel_id=1, source_target_pairs={{0,2},{1,3},{2,0},{3,1},{4,6},{5,7},{6,4},{7,5},{8,10},{9,11},{10,... | collective-permute-start | bytes 368648 | tf_op jit(solution)/shard_map/ppermute | solution.py:194
  16.0 4.2 %collective-permute-start.4 = (f32[10,8,768]{2,1,0:T(8,128)S(1)}, f32[10,8,768]{2,1,0:T(8,128)S(1)}, u32[]{:S(2)}, u32[]{:S(2)}) collective-permute-start(f32[10,8,768]{2,1,0:T(8,128)S(1)} %pad_maximum_fusion.here), channel_id=1, source_target_pairs={{0,1},{1,0},{2,3},{3,2},{4,5},{5,4},{6,7},{7,6},{8,9},{9,8},{10,11... | collective-permute-start | bytes 737288 | tf_op jit(solution)/shard_map/ppermute | solution.py:196

commit v2 on v1

v2 whole, which is shorter than its diff:
```python
import functools
import math

import jax
import jax.numpy as jnp
from jax import lax
from jax.experimental import pallas as pl
from jax.experimental.pallas import tpu as pltpu
from jax.sharding import PartitionSpec as P

FIL = 8
CORE_SQUARE = 0.04
AGE_STEP = 0.25
LISTED = 3
TILE = 256
TERMS = 96
SUMS = 32
F32, BF16 = jnp.float32, jnp.bfloat16
VMEM = pl.BlockSpec(memory_space=pltpu.VMEM)
SMEM = pl.BlockSpec(memory_space=pltpu.SMEM)
ANY = pl.BlockSpec(memory_space=pl.ANY)
PARAMS = pltpu.CompilerParams(vmem_limit_bytes=32 * 2**20)


def split(value):
    high = value.astype(BF16).astype(F32)
    rest = value - high
    middle = rest.astype(BF16).astype(F32)
    return high, middle, rest - middle


def point_factors(points):
    count = points.shape[1]
    zeros = lambda rows: jnp.zeros((rows, count), F32)
    terms = split(-2.0 * points)
    squared = split(jnp.sum(points * points, axis=0, keepdims=True))
    one = jnp.ones((1, count), F32)
    both = []
    for end in (False, True):
        rows = []
        for term in (0, 1, 2, 0, 1, 2, 0, 1):
            rows += [zeros(3), terms[term], zeros(2)] if end else [terms[term], zeros(5)]
        for _ in range(3):
            rows += [zeros(1), one, zeros(6)] if end else [one, zeros(7)]
        rows += [*squared, zeros(5)]
        both.append(jnp.concatenate(rows, axis=0).T.astype(BF16))
    return jnp.concatenate(both, axis=0)


def segment_factors(block):
    one = jnp.ones((1, block.shape[1]), F32)
    zero = jnp.zeros_like(one)
    start = [block[i : i + 1] for i in range(3)]
    end = [block[i : i + 1] for i in range(3, 6)]
    scale = block[6:7] * (0.5 / math.pi)
    along = [a - b for a, b in zip(start, end)]
    moment = [
        start[1] * end[2] - start[2] * end[1],
        start[2] * end[0] - start[0] * end[2],
        start[0] * end[1] - start[1] * end[0],
    ]
    square = lambda v: v[0] * v[0] + v[1] * v[1] + v[2] * v[2]
    norms = jnp.concatenate(
        [square(start) + CORE_SQUARE, square(end) + CORE_SQUARE] + [zero] * 6, axis=0
    )
    high, middle, low = split(block)
    constant = jnp.concatenate([one] * 3 + [zero] * 5, axis=0)
    distance = jnp.concatenate(
        [high, high, high, middle, middle, middle, low, low, *split(norms), constant], axis=0
    ).astype(BF16)
    weights = jnp.concatenate([scale * v for v in along + moment] + [zero] * 2, axis=0)
    cross = jnp.concatenate([*split(weights), jnp.zeros_like(weights)], axis=0).astype(BF16)
    return distance, cross, square(along) + 2.0 * CORE_SQUARE


def add_tile(factors, distance, cross, length, total):
    points = factors.shape[0] // 2
    squared = jnp.dot(factors, distance, preferred_element_type=F32)
    squared_one, squared_two = squared[:points], squared[points:]
    inverse_one, inverse_two = lax.rsqrt(squared_one), lax.rsqrt(squared_two)
    norms = squared_one * inverse_one + squared_two * inverse_two
    factor = (inverse_one + inverse_two) * pltpu.reciprocal(norms * norms - length, approx=True)
    high = factor.astype(BF16)
    low = (factor - high.astype(F32)).astype(BF16)
    contract = (((1,), (1,)), ((), ()))
    return (
        total
        + lax.dot_general(cross, high, contract, preferred_element_type=F32)
        + lax.dot_general(cross, low, contract, preferred_element_type=F32)
    )


def add_wake(factors, wake, held, total):
    for distance, cross, length in held:
        for tile in range(distance.shape[2] // TILE):
            at = pl.ds(tile * TILE, TILE)
            total = add_tile(
                factors, distance[wake, :, at], cross[wake, :, at], length[wake, :, at], total
            )
    return total


def prepare(blocks, buffers, wake):
    distance, cross, length = buffers
    for part, block in enumerate(blocks):
        size = block.shape[1]
        at = pl.ds(part * size, size)
        distance[wake, :, at], cross[wake, :, at], length[wake, :, at] = segment_factors(block)


def used_wakes(mask):
    return mask[0, 0] + mask[0, 1] + mask[0, 2]


def slot_of(upstream, wake, group):
    listed = jnp.where(wake == 0, upstream[0, 0], jnp.where(wake == 1, upstream[0, 1], upstream[0, 2]))
    return lax.rem(listed, group) ^ lax.rem(lax.axis_index("row"), group)


def velocity(where_at, total):
    sums = total[0:8] + total[8:16] + total[16:24]
    x, y, z = where_at[0:1], where_at[1:2], where_at[2:3]
    dx, dy, dz = sums[0:1], sums[1:2], sums[2:3]
    return jnp.concatenate(
        [
            y * dz - z * dy + sums[3:4] + 1.0,
            z * dx - x * dz + sums[4:5],
            x * dy - y * dx + sums[5:6],
        ],
        axis=0,
    )


def pack_kernel(nodes, segments, circulation, packed, semaphores):
    count = nodes.shape[2]
    copies = [
        (circulation, packed.at[6:7]),
        *[(segments.at[i], packed.at[i : i + 1]) for i in range(6)],
        *[(nodes.at[i], packed.at[7:8, i * count : (i + 1) * count]) for i in range(3)],
    ]
    packed[7:8] = jnp.zeros((1, packed.shape[1]), F32)
    started = [
        pltpu.make_async_copy(source, target, semaphores.at[i])
        for i, (source, target) in enumerate(copies)
    ]
    for copy in started:
        copy.start()
    for copy in started:
        copy.wait()


def own_kernel(count, here, there, extended_ref, factors_ref, distance, cross, length, total_ref):
    half = here.shape[0]
    bands = 2 * half
    blocks = [here[i] for i in range(half)] + [there[i] for i in range(half)]
    node_block = lambda block: jnp.concatenate(
        [block[7:8, i * count : (i + 1) * count] for i in range(3)], axis=0
    )
    band = lax.axis_index("band")
    points = node_block(blocks[0])
    root = points[:, :FIL]
    halo = jnp.concatenate([root, root], axis=1)
    for part in range(1, bands):
        flip = sum(bands >> (bit + 1) for bit in range(bands.bit_length()) if part >> bit & 1)
        halo = jnp.where(band ^ flip == band - 1, node_block(blocks[part])[:, -2 * FIL :], halo)
    extended = jnp.concatenate([halo, points], axis=1)
    extended_ref[...] = extended
    factors = point_factors(extended)
    factors_ref[...] = factors
    prepare(blocks, (distance, cross, length), 0)
    total_ref[...] = add_wake(factors, 0, [(distance, cross, length)], jnp.zeros(total_ref.shape, F32))


def stage_kernel(group, upstream, mask, blocks, factors_ref, before, distance, cross, length, total_ref):
    parts = blocks.shape[0] // group
    factors = factors_ref[...]

    def one_wake(wake, total):
        slot = slot_of(upstream, wake, group)
        prepare([blocks[part * group + slot] for part in range(parts)], (distance, cross, length), wake)
        return add_wake(factors, wake, [(distance, cross, length)], total)

    total_ref[...] = lax.fori_loop(0, used_wakes(mask), one_wake, before[...])


def last_kernel(group, stages, upstream, mask, blocks, extended_ref, factors_ref, before, *refs):
    own, earlier = refs[:3], [refs[3 * i : 3 * i + 3] for i in range(1, stages + 1)]
    updated_ref, first_ref, distance, cross, length, results, semaphores = refs[3 * stages + 3 :]
    parts = blocks.shape[0] // group
    used = used_wakes(mask)
    factors = factors_ref[...]
    newest = (distance, cross, length)

    def first_pass(wake, total):
        slot = slot_of(upstream, wake, group)
        prepare([blocks[part * group + slot] for part in range(parts)], newest, wake)
        return add_wake(factors, wake, [newest], total)

    extended = extended_ref[...]
    total = lax.fori_loop(0, used, first_pass, before[...])
    first = velocity(extended, total)
    results[0] = first[:, 2 * FIL :]
    send_first = [
        pltpu.make_async_copy(results.at[0, i : i + 1], first_ref.at[i], semaphores.at[0, i])
        for i in range(3)
    ]
    for copy in send_first:
        copy.start()

    def shifted(field):
        return jnp.concatenate([field[:, :FIL], field[:, :-FIL]], axis=1)

    lane = lax.broadcasted_iota(jnp.int32, extended.shape, 1)
    at_start = lax.axis_index("band") == 0
    kept = (lane < FIL) | (at_start & (lane >= 2 * FIL) & (lane < 3 * FIL))
    pair = first + shifted(first)
    previous = shifted(extended)
    predicted = jnp.where(kept, extended, previous + AGE_STEP * 0.5 * pair)
    moved = point_factors(predicted)
    total = add_wake(moved, 0, [own], jnp.zeros_like(total))
    total = lax.fori_loop(
        0, used, lambda wake, total: add_wake(moved, wake, [*earlier, newest], total), total
    )
    second = velocity(predicted, total)
    pair = pair + second + shifted(second)
    updated = (
        previous + AGE_STEP * 0.25 * pair - (extended - 2.0 * previous + shifted(previous)) / 6.0
    )
    results[1] = jnp.where(kept, extended, updated)[:, 2 * FIL :]
    send_updated = [
        pltpu.make_async_copy(results.at[1, i : i + 1], updated_ref.at[i], semaphores.at[1, i])
        for i in range(3)
    ]
    for copy in send_updated:
        copy.start()
    for copy in send_first + send_updated:
        copy.wait()


def buffers(wakes, segs):
    shapes = ((TERMS, segs), BF16), ((SUMS, segs), BF16), ((1, segs), F32)
    return [((wakes, *shape), dtype) for shape, dtype in shapes]


def outs(*specs):
    return tuple(jax.ShapeDtypeStruct(shape, dtype) for shape, dtype in specs)


def cost(points, segs):
    pairs = points * segs
    return pl.CostEstimate(flops=500 * pairs, bytes_accessed=400 * segs, transcendentals=3 * pairs)


def local(nodes, segments, circulation, upstream, upstream_mask):
    rows, bands = lax.axis_size("row"), lax.axis_size("band")
    group = min(8, rows // 2)
    seg_count = segments.shape[2]
    count = nodes.shape[2]
    points = count + 2 * FIL
    sums = ((SUMS, points), F32)

    own = pl.pallas_call(
        pack_kernel,
        out_shape=jax.ShapeDtypeStruct((8, seg_count), F32),
        in_specs=[ANY] * 3,
        out_specs=VMEM,
        scratch_shapes=[pltpu.SemaphoreType.DMA((10,))],
    )(nodes.transpose(1, 0, 2), segments.transpose(1, 0, 2), circulation)[None]

    wakes, bit = own, 1
    while bit < group // 2:
        route = [(i, i ^ bit) for i in range(rows - group)]
        wakes = jnp.concatenate([wakes, lax.ppermute(wakes, "row", route)])
        bit *= 2
    arrived = [
        lax.ppermute(wakes, "row", [(i, (i ^ flip) + group) for i in range(rows - group)])
        for flip in ((0, bit) if group > 1 else (0,))
    ]

    def across(blocks, bit):
        return lax.ppermute(blocks, "band", [(i, i ^ bit) for i in range(bands)])

    here, bit = own, bands // 2
    while bit > 1:
        here = jnp.concatenate([here, across(here, bit)])
        bit //= 2
    there = across(here, 1)
    segs = bands * seg_count
    extended, factors, *held = pl.pallas_call(
        functools.partial(own_kernel, count),
        out_shape=outs(((3, points), F32), ((2 * points, TERMS), BF16), *buffers(1, segs), sums),
        in_specs=[VMEM] * 2,
        out_specs=(VMEM,) * 6,
        compiler_params=PARAMS,
        cost_estimate=cost(points, segs),
    )(here, there)
    total = held.pop()

    *arrived, total = lax.optimization_barrier((*arrived, total))
    here = fresh = jnp.concatenate(arrived)
    bit = bands // 2
    stages = 0
    while bit:
        following = across(here, bit)
        new_segs = fresh.shape[0] // group * seg_count
        *prepared, total = pl.pallas_call(
            functools.partial(stage_kernel, group),
            out_shape=outs(*buffers(LISTED, new_segs), sums),
            in_specs=[SMEM] * 2 + [VMEM] * 3,
            out_specs=(VMEM,) * 4,
            compiler_params=PARAMS,
            cost_estimate=cost(points, LISTED * new_segs),
        )(upstream, upstream_mask, fresh, factors, total)
        held += prepared
        stages += 1
        if bit > 1:
            following, total = lax.optimization_barrier((following, total))
        here, fresh = jnp.concatenate([here, following]), following
        bit //= 2

    new_segs = fresh.shape[0] // group * seg_count
    out = ((3, 1, count), F32)
    updated, first = pl.pallas_call(
        functools.partial(last_kernel, group, stages),
        out_shape=outs(out, out),
        in_specs=[SMEM] * 2 + [VMEM] * (4 + 3 * (stages + 1)),
        out_specs=(ANY,) * 2,
        scratch_shapes=[
            *[pltpu.VMEM(shape, dtype) for shape, dtype in buffers(LISTED, new_segs)],
            pltpu.VMEM((2, 3, count), F32),
            pltpu.SemaphoreType.DMA((2, 3)),
        ],
        compiler_params=PARAMS,
        cost_estimate=cost(points, 4 * segs),
    )(upstream, upstream_mask, fresh, extended, factors, total, *held)
    return updated.transpose(1, 0, 2), first.transpose(1, 0, 2)


def solution(mesh):
    placed = (
        P("row", None, "band"),
        P("row", None, "band"),
        P("row", "band"),
        P("row", None),
        P("row", None),
    )
    return jax.shard_map(
        local,
        mesh=mesh,
        in_specs=placed,
        out_specs=(P("row", None, "band"), P("row", None, "band")),
        check_vma=False,
    )
```

time: 33.3 us -> 34.6 us (1.039)
  Pallas kernels: 11.6 us -> 16.6 us
  waiting for transfers between devices: 10.5 us -> 7.25 us
  local copies, waits for them, and re-layouts: 2.56 us -> 0.02 us
  starting transfers between devices: 7.58 us -> 8.97 us
  other arithmetic: 0.05 us -> 0.76 us
    pallas_call x1 -> x5, Pallas kernels: 11.6 us -> 16.6 us  [the longest x1 9.02 us: local(): pl.pallas_call(functools.partial(last_kernel, group, stages), out_shape=o...]
    ppermute x2 -> x4, waiting for transfers between devices: 3.66 us -> 1.45 us  [across(): return lax.ppermute(blocks, 'band', [(i, i ^ bit) for i in range(bands)])]
    unnamed x9 -> x5, local copies, waits for them, and re-layouts: 1.43 us -> 0.02 us
    ppermute x2 -> x4, starting transfers between devices: 4.34 us -> 5.75 us  [across(): return lax.ppermute(blocks, 'band', [(i, i ^ bit) for i in range(bands)])]
    pallas_call x2 -> x0, local copies, waits for them, and re-layouts: 1.13 us -> none  [local(): pl.pallas_call(functools.partial(kernel, bands, group), out_shape=(out, o...]
    ppermute x2, waiting for transfers between devices: 6.81 us -> 5.8 us  [local(): lax.ppermute(wakes, 'row', [(i, (i ^ flip) + group) for i in range(rows -...]
    concatenate x3 -> x2, other arithmetic: 0.04 us -> 0.76 us  [the longest x1 0.75 us: local(): here = jnp.concatenate([here, across(here, bit)])]
  transfers between devices with their start and end apart: 5 -> 7, of which waited for: 4 -> 4; matrix products, arithmetic and copies ran while one was open for 0% -> 0% of each run, Pallas kernels for 0% -> 18%
where the time goes in v2:
time: 34.6 us; the launch traced here: 34.3 us
  Pallas kernels  16.6 us (48%)
  starting transfers between devices  8.97 us (26%)
  waiting for transfers between devices  7.25 us (21%)
  other arithmetic  0.76 us (2%)
  between operations  0.72 us (2%)
    pallas_call x1, Pallas kernels, local(): pl.pallas_call(functools.partial(last_kernel, group, stages), out_shape=o...  9.02 us
    ppermute x2, waiting for transfers between devices, local(): lax.ppermute(wakes, 'row', [(i, (i ^ flip) + group) for i in range(rows -...  5.8 us
    ppermute x4, starting transfers between devices, across(): return lax.ppermute(blocks, 'band', [(i, i ^ bit) for i in range(bands)])  5.75 us
    pallas_call x2, Pallas kernels, local(): pl.pallas_call(functools.partial(stage_kernel, group), out_shape=outs(*bu...  4.52 us
    ppermute x2, starting transfers between devices, local(): lax.ppermute(wakes, 'row', [(i, (i ^ flip) + group) for i in range(rows -...  2.57 us
    pallas_call x1, Pallas kernels, local(): pl.pallas_call(functools.partial(own_kernel, count), out_shape=outs(((3,...  1.55 us
    pallas_call x1, Pallas kernels, local(): pl.pallas_call(pack_kernel, out_shape=jax.ShapeDtypeStruct((8, seg_count)...  1.48 us
    ppermute x4, waiting for transfers between devices, across(): return lax.ppermute(blocks, 'band', [(i, i ^ bit) for i in range(bands)])  1.45 us
  transfers between devices with their start and end apart: 7, of which 4 were waited for; matrix products, arithmetic and copies ran while one was open for 0% of the time, Pallas kernels for 18%

profile of v2, /device:TPU:29, one launch (start us, length us, event | category | flops | bytes accessed | tf_op | source)
XLA Modules:
  0.0 34.3 jit_solution(2632128902868073961)
XLA Ops:
  0.6 1.5 %shard_map.68 = f32[8,768]{1,0:T(8,128)} custom-call(f32[3,1,128]{2,1,0:T(1,128)} %bitcast.9, f32[6,1,768]{2,1,0:T(1,128)} %bitcast.8, f32[1,768]{1,0:T(1,128)} %circulation.1), custom_call_target="tpu_custom_call" | custom-call | tf_op jit(solution)/shard_map/pallas_call | solution.py:262
  2.1 1.3 %collective-permute-start.3 = (f32[1,8,768]{2,1,0:T(8,128)}, f32[1,8,768]{2,1,0:T(8,128)S(1)}, u32[]{:S(2)}, u32[]{:S(2)}) collective-permute-start(f32[1,8,768]{2,1,0:T(8,128)} %bitcast.5), channel_id=1, source_target_pairs={{0,2},{1,3},{2,0},{3,1},{4,6},{5,7},{6,4},{7,5},{8,10},{9,11},{10,... | collective-permute-start | bytes 73736 | tf_op jit(solution)/shard_map/ppermute | solution.py:281
  3.4 0.7 %collective-permute-start = (f32[1,8,768]{2,1,0:T(8,128)}, f32[1,8,768]{2,1,0:T(8,128)S(1)}, u32[]{:S(2)}, u32[]{:S(2)}) collective-permute-start(f32[1,8,768]{2,1,0:T(8,128)} %bitcast.6), channel_id=1, source_target_pairs={{0,4},{4,0},{8,12},{12,8},{1,5},{5,1},{9,13},{13,9},{2,6},{6,2},{1... | collective-permute-start | bytes 73736 | tf_op jit(solution)/shard_map/ppermute | solution.py:273
  4.1 1.0 %collective-permute-done.3 = f32[1,8,768]{2,1,0:T(8,128)S(1)} collective-permute-done((f32[1,8,768]{2,1,0:T(8,128)}, f32[1,8,768]{2,1,0:T(8,128)S(1)}, u32[]{:S(2)}, u32[]{:S(2)}) %collective-permute-start.3) | collective-permute-done | bytes 24608 | tf_op jit(solution)/shard_map/ppermute | solution.py:281
  5.1 0.0 collective-permute-done
  5.1 0.7 %pad_maximum_fusion.1 = (f32[2,8,768]{2,1,0:T(8,128)S(1)}, f32[2,8,768]{2,1,0:T(8,128)S(1)}) fusion(f32[1,8,768]{2,1,0:T(8,128)} %bitcast.7, f32[1,8,768]{2,1,0:T(8,128)S(1)} %collective-permute-done.3, f32[1,8,768]{2,1,0:T(8,128)S(1)} %collective-permute-done), kind=kLoop, calls=%fused_computation.1 | loop fusion | flops 24576 | bytes 172032 | tf_op jit(solution)/shard_map/concatenate | solution.py:285
  5.8 1.8 %collective-permute-start.4 = (f32[2,8,768]{2,1,0:T(8,128)S(1)}, f32[2,8,768]{2,1,0:T(8,128)S(1)}, u32[]{:S(2)}, u32[]{:S(2)}) collective-permute-start(f32[2,8,768]{2,1,0:T(8,128)S(1)} %get-tuple-element.44.here), channel_id=1, source_target_pairs={{0,1},{1,0},{2,3},{3,2},{4,5},{5,4},{6,7},{7,6},{8,9},{9,8},{10,11... | collective-permute-start | bytes 147464 | tf_op jit(solution)/shard_map/ppermute | solution.py:281
  7.6 1.3 %collective-permute-start.2 = (f32[2,8,768]{2,1,0:T(8,128)S(1)}, f32[2,8,768]{2,1,0:T(8,128)S(1)}, u32[]{:S(2)}, u32[]{:S(2)}) collective-permute-start(f32[2,8,768]{2,1,0:T(8,128)S(1)} %get-tuple-element.45), channel_id=1, source_target_pairs={{0,24},{4,28},{8,16},{12,20},{1,25},{5,29},{9,17},{13,21},{2,26},{... | collective-permute-start | bytes 147464 | tf_op jit(solution)/shard_map/ppermute | solution.py:276
  8.9 1.3 %collective-permute-start.1 = (f32[2,8,768]{2,1,0:T(8,128)S(1)}, f32[2,8,768]{2,1,0:T(8,128)S(1)}, u32[]{:S(2)}, u32[]{:S(2)}) collective-permute-start(f32[2,8,768]{2,1,0:T(8,128)S(1)} %get-tuple-element.45), channel_id=1, source_target_pairs={{0,16},{4,20},{8,24},{12,28},{1,17},{5,21},{9,25},{13,29},{2,18},{... | collective-permute-start | bytes 147464 | tf_op jit(solution)/shard_map/ppermute | solution.py:276
  10.2 0.0 collective-permute-done.4.there
  10.2 1.5 %shard_map.69 = (f32[3,144]{1,0:T(4,128)S(1)}, bf16[288,96]{1,0:T(8,128)(2,1)S(1)}, bf16[1,96,3072]{2,1,0:T(8,128)(2,1)S(1)}, bf16[1,32,3072]{2,1,0:T(8,128)(2,1...) custom-call(f32[2,8,768]{2,1,0:T(8,128)S(1)} %get-tuple-element.44.here, ...), custom_call_target="tpu_custom_call" | custom-call | flops 221184000 | bytes 1228800 | tf_op jit(solution)/shard_map/pallas_call | solution.py:289
  11.8 2.9 %collective-permute-done.2 = f32[2,8,768]{2,1,0:T(8,128)S(1)} collective-permute-done((f32[2,8,768]{2,1,0:T(8,128)S(1)}, f32[2,8,768]{2,1,0:T(8,128)S(1)}, u32[]{:S(2)}, u32[]{:S(2)}) %collective-permute-start.2) | collective-permute-done | bytes 49184 | tf_op jit(solution)/shard_map/ppermute | solution.py:276
  14.7 2.9 %collective-permute-done.1 = f32[2,8,768]{2,1,0:T(8,128)S(1)} collective-permute-done((f32[2,8,768]{2,1,0:T(8,128)S(1)}, f32[2,8,768]{2,1,0:T(8,128)S(1)}, u32[]{:S(2)}, u32[]{:S(2)}) %collective-permute-start.1) | collective-permute-done | bytes 49184 | tf_op jit(solution)/shard_map/ppermute | solution.py:276
  17.6 0.0 copy-start
  17.6 0.0 copy-start.1
  17.6 0.8 %collective-permute-start.5 = (f32[4,8,768]{2,1,0:T(8,128)S(1)}, f32[4,8,768]{2,1,0:T(8,128)S(1)}, u32[]{:S(2)}, u32[]{:S(2)}) collective-permute-start(f32[4,8,768]{2,1,0:T(8,128)S(1)} %constant_dynamic-update-slice_fusion.blocks), channel_id=1, source_target_pairs={{0,2},{1,3},{2,0},{3,1},{4,6},{5,7},{6,4},{7,5},{8,10},{9,11},{10,... | collective-permute-start | bytes 294920 | tf_op jit(solution)/shard_map/ppermute | solution.py:281
  18.5 0.0 copy-done
  18.5 0.0 copy-done.1
  18.5 2.3 %shard_map.70 = (bf16[3,96,768]{2,1,0:T(8,128)(2,1)S(1)}, bf16[3,32,768]{2,1,0:T(8,128)(2,1)S(1)}, f32[3,1,768]{2,1,0:T(1,128)S(1)}, f32[32,144]{1,0:T(8,128)S(1)}) custom-call(s32[1,3]{1,0:T(1,128)S(1)} %copy-done, s32[1,3]{1,0:T(1,128)S(1)} %copy-done.1, f32[4,8,768]{2,1,0:T(8,128)S(1)} %constant_dynamic-update-slice_fusion.blocks, ...), custom_call_target="tpu_custom_call" | custom-call | flops 165888000 | bytes 921600 | tf_op jit(solution)/shard_map/pallas_call | solution.py:306
  20.7 0.4 %collective-permute-done.5.blocks = f32[4,8,768]{2,1,0:T(8,128)S(1)} collective-permute-done((f32[4,8,768]{2,1,0:T(8,128)S(1)}, f32[4,8,768]{2,1,0:T(8,128)S(1)}, u32[]{:S(2)}, u32[]{:S(2)}) %collective-permute-start.5) | collective-permute-done | bytes 98336 | tf_op jit(solution)/shard_map/ppermute | solution.py:281
  21.2 1.8 %collective-permute-start.6 = (f32[8,8,768]{2,1,0:T(8,128)S(1)}, f32[8,8,768]{2,1,0:T(8,128)S(1)}, u32[]{:S(2)}, u32[]{:S(2)}) collective-permute-start(f32[8,8,768]{2,1,0:T(8,128)S(1)} %pad_maximum_fusion), channel_id=1, source_target_pairs={{0,1},{1,0},{2,3},{3,2},{4,5},{5,4},{6,7},{7,6},{8,9},{9,8},{10,11... | collective-permute-start | bytes 589832 | tf_op jit(solution)/shard_map/ppermute | solution.py:281
  23.0 2.3 %shard_map.71 = (bf16[3,96,768]{2,1,0:T(8,128)(2,1)S(1)}, bf16[3,32,768]{2,1,0:T(8,128)(2,1)S(1)}, f32[3,1,768]{2,1,0:T(1,128)S(1)}, f32[32,144]{1,0:T(8,128)S(1)}) custom-call(s32[1,3]{1,0:T(1,128)S(1)} %copy-done, s32[1,3]{1,0:T(1,128)S(1)} %copy-done.1, f32[4,8,768]{2,1,0:T(8,128)S(1)} %collective-permute-done.5.blocks, ...), custom_call_target="tpu_custom_call" | custom-call | flops 165888000 | bytes 921600 | tf_op jit(solution)/shard_map/pallas_call | solution.py:306
  25.3 0.0 collective-permute-done.6.blocks
  25.3 9.0 %shard_map.72 = (f32[3,1,128]{2,1,0:T(1,128)}, f32[3,1,128]{2,1,0:T(1,128)}) custom-call(s32[1,3]{1,0:T(1,128)S(1)} %copy-done, s32[1,3]{1,0:T(1,128)S(1)} %copy-done.1, f32[8,8,768]{2,1,0:T(8,128)S(1)} %collective-permute-done.6.blocks, f32[3,144]{1,0:T(4,128)S(1)} %get-tuple-element.30.extended_ref, bf16[288,96]{1,0:T(8,128)(2,1)S(1)} %get-tuple-element.26.factors_ref, ...), custom_call_target="tpu_custom_call" | custom-call | flops 884736000 | bytes 4915200 | tf_op jit(solution)/shard_map/pallas_call | solution.py:323
  (3 shorter events, 0.0 us)
Async XLA Ops:
  2.1 3.0 %collective-permute-start.3 = (f32[1,8,768]{2,1,0:T(8,128)}, f32[1,8,768]{2,1,0:T(8,128)S(1)}, u32[]{:S(2)}, u32[]{:S(2)}) collective-permute-start(f32[1,8,768]{2,1,0:T(8,128)} %bitcast.5), channel_id=1, source_target_pairs={{0,2},{1,3},{2,0},{3,1},{4,6},{5,7},{6,4},{7,5},{8,10},{9,11},{10,... | collective-permute-start | bytes 73736 | tf_op jit(solution)/shard_map/ppermute | solution.py:281
  3.4 1.7 %collective-permute-start = (f32[1,8,768]{2,1,0:T(8,128)}, f32[1,8,768]{2,1,0:T(8,128)S(1)}, u32[]{:S(2)}, u32[]{:S(2)}) collective-permute-start(f32[1,8,768]{2,1,0:T(8,128)} %bitcast.6), channel_id=1, source_target_pairs={{0,4},{4,0},{8,12},{12,8},{1,5},{5,1},{9,13},{13,9},{2,6},{6,2},{1... | collective-permute-start | bytes 73736 | tf_op jit(solution)/shard_map/ppermute | solution.py:273
  5.8 4.4 %collective-permute-start.4 = (f32[2,8,768]{2,1,0:T(8,128)S(1)}, f32[2,8,768]{2,1,0:T(8,128)S(1)}, u32[]{:S(2)}, u32[]{:S(2)}) collective-permute-start(f32[2,8,768]{2,1,0:T(8,128)S(1)} %get-tuple-element.44.here), channel_id=1, source_target_pairs={{0,1},{1,0},{2,3},{3,2},{4,5},{5,4},{6,7},{7,6},{8,9},{9,8},{10,11... | collective-permute-start | bytes 147464 | tf_op jit(solution)/shard_map/ppermute | solution.py:281
  7.6 7.0 %collective-permute-start.2 = (f32[2,8,768]{2,1,0:T(8,128)S(1)}, f32[2,8,768]{2,1,0:T(8,128)S(1)}, u32[]{:S(2)}, u32[]{:S(2)}) collective-permute-start(f32[2,8,768]{2,1,0:T(8,128)S(1)} %get-tuple-element.45), channel_id=1, source_target_pairs={{0,24},{4,28},{8,16},{12,20},{1,25},{5,29},{9,17},{13,21},{2,26},{... | collective-permute-start | bytes 147464 | tf_op jit(solution)/shard_map/ppermute | solution.py:276
  8.9 8.7 %collective-permute-start.1 = (f32[2,8,768]{2,1,0:T(8,128)S(1)}, f32[2,8,768]{2,1,0:T(8,128)S(1)}, u32[]{:S(2)}, u32[]{:S(2)}) collective-permute-start(f32[2,8,768]{2,1,0:T(8,128)S(1)} %get-tuple-element.45), channel_id=1, source_target_pairs={{0,16},{4,20},{8,24},{12,28},{1,17},{5,21},{9,25},{13,29},{2,18},{... | collective-permute-start | bytes 147464 | tf_op jit(solution)/shard_map/ppermute | solution.py:276
  17.6 0.9 %copy-start = (s32[1,3]{1,0:T(1,128)S(1)}, s32[1,3]{1,0:T(1,128)}, u32[]{:S(2)}) copy-start(s32[1,3]{1,0:T(1,128)} %upstream.5) | copy-start | bytes 40
  17.6 0.9 %copy-start.1 = (s32[1,3]{1,0:T(1,128)S(1)}, s32[1,3]{1,0:T(1,128)}, u32[]{:S(2)}) copy-start(s32[1,3]{1,0:T(1,128)} %mask.5) | copy-start | bytes 40
  17.6 3.5 %collective-permute-start.5 = (f32[4,8,768]{2,1,0:T(8,128)S(1)}, f32[4,8,768]{2,1,0:T(8,128)S(1)}, u32[]{:S(2)}, u32[]{:S(2)}) collective-permute-start(f32[4,8,768]{2,1,0:T(8,128)S(1)} %constant_dynamic-update-slice_fusion.blocks), channel_id=1, source_target_pairs={{0,2},{1,3},{2,0},{3,1},{4,6},{5,7},{6,4},{7,5},{8,10},{9,11},{10,... | collective-permute-start | bytes 294920 | tf_op jit(solution)/shard_map/ppermute | solution.py:281
  21.2 4.1 %collective-permute-start.6 = (f32[8,8,768]{2,1,0:T(8,128)S(1)}, f32[8,8,768]{2,1,0:T(8,128)S(1)}, u32[]{:S(2)}, u32[]{:S(2)}) collective-permute-start(f32[8,8,768]{2,1,0:T(8,128)S(1)} %pad_maximum_fusion), channel_id=1, source_target_pairs={{0,1},{1,0},{2,3},{3,2},{4,5},{5,4},{6,7},{7,6},{8,9},{9,8},{10,11... | collective-permute-start | bytes 589832 | tf_op jit(solution)/shard_map/ppermute | solution.py:281

commit v3 on v2

--- a/solution.py
+++ b/solution.py
@@ -17,7 +17,6 @@
 SUMS = 32
 F32, BF16 = jnp.float32, jnp.bfloat16
 VMEM = pl.BlockSpec(memory_space=pltpu.VMEM)
-SMEM = pl.BlockSpec(memory_space=pltpu.SMEM)
 ANY = pl.BlockSpec(memory_space=pl.ANY)
 PARAMS = pltpu.CompilerParams(vmem_limit_bytes=32 * 2**20)
 
@@ -109,11 +108,12 @@
 
 
 def used_wakes(mask):
-    return mask[0, 0] + mask[0, 1] + mask[0, 2]
+    return jnp.sum(mask[...])
 
 
 def slot_of(upstream, wake, group):
-    listed = jnp.where(wake == 0, upstream[0, 0], jnp.where(wake == 1, upstream[0, 1], upstream[0, 2]))
+    lane = lax.broadcasted_iota(jnp.int32, upstream.shape, 1)
+    listed = jnp.sum(jnp.where(lane == wake, upstream[...], 0))
     return lax.rem(listed, group) ^ lax.rem(lax.axis_index("row"), group)
 
 
@@ -150,9 +150,8 @@
 
 
 def own_kernel(count, here, there, extended_ref, factors_ref, distance, cross, length, total_ref):
-    half = here.shape[0]
-    bands = 2 * half
-    blocks = [here[i] for i in range(half)] + [there[i] for i in range(half)]
+    bands = 1 + there.shape[0]
+    blocks = [here[0]] + [there[i] for i in range(bands - 1)]
     node_block = lambda block: jnp.concatenate(
         [block[7:8, i * count : (i + 1) * count] for i in range(3)], axis=0
     )
@@ -160,9 +159,8 @@
     points = node_block(blocks[0])
     root = points[:, :FIL]
     halo = jnp.concatenate([root, root], axis=1)
-    for part in range(1, bands):
-        flip = sum(bands >> (bit + 1) for bit in range(bands.bit_length()) if part >> bit & 1)
-        halo = jnp.where(band ^ flip == band - 1, node_block(blocks[part])[:, -2 * FIL :], halo)
+    for flip in range(1, bands):
+        halo = jnp.where(band ^ flip == band - 1, node_block(blocks[flip])[:, -2 * FIL :], halo)
     extended = jnp.concatenate([halo, points], axis=1)
     extended_ref[...] = extended
     factors = point_factors(extended)
@@ -171,29 +169,65 @@
     total_ref[...] = add_wake(factors, 0, [(distance, cross, length)], jnp.zeros(total_ref.shape, F32))
 
 
-def stage_kernel(group, upstream, mask, blocks, factors_ref, before, distance, cross, length, total_ref):
-    parts = blocks.shape[0] // group
+def near_kernel(group, upstream, mask, blocks, factors_ref, before, distance, cross, length, total_ref):
+    low = group // 2
     factors = factors_ref[...]
+    size = blocks.shape[2]
+    view = tuple(ref.at[:, :, :size] for ref in (distance, cross, length))
 
     def one_wake(wake, total):
         slot = slot_of(upstream, wake, group)
-        prepare([blocks[part * group + slot] for part in range(parts)], (distance, cross, length), wake)
-        return add_wake(factors, wake, [(distance, cross, length)], total)
+
+        def add(total):
+            prepare([blocks[slot // low]], view, wake)
+            return add_wake(factors, wake, [view], total)
+
+        return lax.cond(lax.rem(slot, low) == 0, add, lambda total: total, total)
 
     total_ref[...] = lax.fori_loop(0, used_wakes(mask), one_wake, before[...])
 
 
-def last_kernel(group, stages, upstream, mask, blocks, extended_ref, factors_ref, before, *refs):
-    own, earlier = refs[:3], [refs[3 * i : 3 * i + 3] for i in range(1, stages + 1)]
-    updated_ref, first_ref, distance, cross, length, results, semaphores = refs[3 * stages + 3 :]
-    parts = blocks.shape[0] // group
+def far_kernel(
+    group, parts, upstream, mask, far, factors_ref, before, *refs
+):
+    low = group // 2
+    tops = group // low
+    distance, cross, length, total_ref = refs[3:]
+    factors = factors_ref[...]
+    size = far.shape[2]
+    view = lambda part: tuple(
+        ref.at[:, :, part * size : (part + 1) * size] for ref in (distance, cross, length)
+    )
+
+    def one_wake(wake, total):
+        slot = slot_of(upstream, wake, group)
+
+        def add(part, total):
+            at = (lax.rem(slot, low) * parts + part) * tops + slot // low - tops
+            prepare([far[at]], view(part), wake)
+            return add_wake(factors, wake, [view(part)], total)
+
+        total = lax.cond(lax.rem(slot, low) == 0, lambda t: t, functools.partial(add, 0), total)
+        for part in range(1, parts):
+            total = add(part, total)
+        return total
+
+    total_ref[...] = lax.fori_loop(0, used_wakes(mask), one_wake, before[...])
+
+
+def last_kernel(group, parts, upstream, mask, blocks, extended_ref, factors_ref, before, *refs):
+    own, earlier = refs[:3], refs[3:6]
+    updated_ref, first_ref, distance, cross, length, results, semaphores = refs[6:]
+    low = group // 2
+    tops = group // low
     used = used_wakes(mask)
     factors = factors_ref[...]
     newest = (distance, cross, length)
 
     def first_pass(wake, total):
         slot = slot_of(upstream, wake, group)
-        prepare([blocks[part * group + slot] for part in range(parts)], newest, wake)
+        at = lambda part: (lax.rem(slot, low) * parts + part) * tops + slot // low
+        prepare([blocks[at(part)] for part in range(parts)], newest, wake)
         return add_wake(factors, wake, [newest], total)
 
     extended = extended_ref[...]
@@ -219,7 +253,7 @@
     moved = point_factors(predicted)
     total = add_wake(moved, 0, [own], jnp.zeros_like(total))
     total = lax.fori_loop(
-        0, used, lambda wake, total: add_wake(moved, wake, [*earlier, newest], total), total
+        0, used, lambda wake, total: add_wake(moved, wake, [earlier, newest], total), total
     )
     second = velocity(predicted, total)
     pair = pair + second + shifted(second)
@@ -261,78 +295,85 @@
 
     own = pl.pallas_call(
         pack_kernel,
-        out_shape=jax.ShapeDtypeStruct((8, seg_count), F32),
+        out_shape=pltpu.VMEM((8, seg_count), F32),
         in_specs=[ANY] * 3,
         out_specs=VMEM,
         scratch_shapes=[pltpu.SemaphoreType.DMA((10,))],
     )(nodes.transpose(1, 0, 2), segments.transpose(1, 0, 2), circulation)[None]
 
-    wakes, bit = own, 1
-    while bit < group // 2:
-        route = [(i, i ^ bit) for i in range(rows - group)]
-        wakes = jnp.concatenate([wakes, lax.ppermute(wakes, "row", route)])
-        bit *= 2
-    arrived = [
-        lax.ppermute(wakes, "row", [(i, (i ^ flip) + group) for i in range(rows - group)])
-        for flip in ((0, bit) if group > 1 else (0,))
-    ]
-
+    low, parts = group // 2, bands // 2
+    tops = group // low
     def across(blocks, bit):
         return lax.ppermute(blocks, "band", [(i, i ^ bit) for i in range(bands)])
 
-    here, bit = own, bands // 2
-    while bit > 1:
-        here = jnp.concatenate([here, across(here, bit)])
-        bit //= 2
-    there = across(here, 1)
+    there = jnp.concatenate([across(own, flip) for flip in range(1, bands)])
+    near = [
+        lax.ppermute(own, "row", [(i, (i ^ flip) + group) for i in range(rows - group)])
+        for flip in range(0, group, low)
+    ]
+
     segs = bands * seg_count
-    extended, factors, *held = pl.pallas_call(
+    extended, factors, *held, total = pl.pallas_call(
         functools.partial(own_kernel, count),
         out_shape=outs(((3, points), F32), ((2 * points, TERMS), BF16), *buffers(1, segs), sums),
         in_specs=[VMEM] * 2,
         out_specs=(VMEM,) * 6,
         compiler_params=PARAMS,
-        cost_estimate=cost(points, segs),
-    )(here, there)
-    total = held.pop()
-
-    *arrived, total = lax.optimization_barrier((*arrived, total))
-    here = fresh = jnp.concatenate(arrived)
-    bit = bands // 2
-    stages = 0
-    while bit:
-        following = across(here, bit)
-        new_segs = fresh.shape[0] // group * seg_count
-        *prepared, total = pl.pallas_call(
-            functools.partial(stage_kernel, group),
-            out_shape=outs(*buffers(LISTED, new_segs), sums),
-            in_specs=[SMEM] * 2 + [VMEM] * 3,
-            out_specs=(VMEM,) * 4,
-            compiler_params=PARAMS,
-            cost_estimate=cost(points, LISTED * new_segs),
-        )(upstream, upstream_mask, fresh, factors, total)
-        held += prepared
-        stages += 1
-        if bit > 1:
-            following, total = lax.optimization_barrier((following, total))
-        here, fresh = jnp.concatenate([here, following]), following
-        bit //= 2
-
-    new_segs = fresh.shape[0] // group * seg_count
+        cost_estimate=cost(1, 1),
+    )(own, there)
+
+    *near, total = lax.optimization_barrier((*near, total))
+    near = jnp.concatenate(near)
+
+    def route(row_flip, band_flip):
+        return [
+            (i * bands + j, (i ^ row_flip) * bands + (j ^ 2 * band_flip))
+            for i in range(group, rows)
+            for j in range(bands)
+        ]
+
+    far = jnp.concatenate(
+        [
+            lax.ppermute(near, ("row", "band"), route(row_flip, band_flip))
+            for row_flip in range(low)
+            for band_flip in range(parts)
+            if row_flip or band_flip
+        ]
+    )
+    *half, total = pl.pallas_call(
+        functools.partial(near_kernel, group),
+        out_shape=outs(*buffers(LISTED, parts * seg_count), sums),
+        in_specs=[VMEM] * 5,
+        out_specs=(VMEM,) * 4,
+        compiler_params=PARAMS,
+        cost_estimate=cost(points, LISTED * seg_count),
+    )(upstream, upstream_mask, near, factors, total)
+    far, total = lax.optimization_barrier((far, total))
+    last = across(jnp.concatenate([near, far]), 1)
+    *half, total = pl.pallas_call(
+        functools.partial(far_kernel, group, parts),
+        out_shape=outs(*buffers(LISTED, parts * seg_count), sums),
+        in_specs=[VMEM] * 8,
+        out_specs=(VMEM,) * 4,
+        input_output_aliases={5: 0, 6: 1, 7: 2},
+        compiler_params=PARAMS,
+        cost_estimate=cost(points, LISTED * seg_count),
+    )(upstream, upstream_mask, far, factors, total, *half)
+
     out = ((3, 1, count), F32)
     updated, first = pl.pallas_call(
-        functools.partial(last_kernel, group, stages),
+        functools.partial(last_kernel, group, parts),
         out_shape=outs(out, out),
-        in_specs=[SMEM] * 2 + [VMEM] * (4 + 3 * (stages + 1)),
+        in_specs=[VMEM] * 12,
         out_specs=(ANY,) * 2,
         scratch_shapes=[
-            *[pltpu.VMEM(shape, dtype) for shape, dtype in buffers(LISTED, new_segs)],
+            *[pltpu.VMEM(shape, dtype) for shape, dtype in buffers(LISTED, parts * seg_count)],
             pltpu.VMEM((2, 3, count), F32),
             pltpu.SemaphoreType.DMA((2, 3)),
         ],
         compiler_params=PARAMS,
         cost_estimate=cost(points, 4 * segs),
-    )(upstream, upstream_mask, fresh, extended, factors, total, *held)
+    )(upstream, upstream_mask, last, extended, factors, total, *held, *half)
     return updated.transpose(1, 0, 2), first.transpose(1, 0, 2)
 
 

time: 34.6 us -> 38.3 us (1.11)
  the two profiles are of different devices: /device:TPU:29 before, /device:TPU:21 now
where the time goes in v3:
time: 38.3 us; the launch traced here: 37.8 us
  starting transfers between devices  16.6 us (43%)
  Pallas kernels  15.8 us (41%)
  waiting for transfers between devices  4.57 us (12%)
  between operations  0.79 us (2%)
    pallas_call x1, Pallas kernels, local(): pl.pallas_call(functools.partial(last_kernel, group, parts), out_shape=ou...  8.94 us
    ppermute x3, starting transfers between devices, local(): lax.ppermute(near, ('row', 'band'), route(row_flip, band_flip))  8.51 us
    ppermute x4, starting transfers between devices, across(): return lax.ppermute(blocks, 'band', [(i, i ^ bit) for i in range(bands)])  5.53 us
    ppermute x2, waiting for transfers between devices, local(): lax.ppermute(own, 'row', [(i, (i ^ flip) + group) for i in range(rows - g...  3.68 us
    pallas_call x1, Pallas kernels, local(): pl.pallas_call(functools.partial(far_kernel, group, parts), out_shape=out...  2.75 us
    ppermute x2, starting transfers between devices, local(): lax.ppermute(own, 'row', [(i, (i ^ flip) + group) for i in range(rows - g...  2.57 us
    pallas_call x1, Pallas kernels, local(): pl.pallas_call(functools.partial(near_kernel, group), out_shape=outs(*buf...  1.67 us
    pallas_call x1, Pallas kernels, local(): pl.pallas_call(functools.partial(own_kernel, count), out_shape=outs(((3,...  1.55 us
  transfers between devices with their start and end apart: 9, of which 3 were waited for; matrix products, arithmetic and copies ran while one was open for 0% of the time, Pallas kernels for 16%

profile of v3, /device:TPU:21, one launch (start us, length us, event | category | flops | bytes accessed | tf_op | source)
XLA Modules:
  0.0 37.8 jit_solution(4861744639726331054)
XLA Ops:
  0.6 0.9 %shard_map.68 = f32[8,768]{1,0:T(8,128)S(1)} custom-call(f32[3,1,128]{2,1,0:T(1,128)} %bitcast.12, f32[6,1,768]{2,1,0:T(1,128)} %bitcast.11, f32[1,768]{1,0:T(1,128)} %circulation.1), custom_call_target="tpu_custom_call" | custom-call | tf_op jit(solution)/shard_map/pallas_call | solution.py:296
  1.5 1.8 %collective-permute-start.4 = (f32[1,8,768]{2,1,0:T(8,128)S(1)}, f32[1,8,768]{2,1,0:T(8,128)S(1)}, u32[]{:S(2)}, u32[]{:S(2)}) collective-permute-start(f32[1,8,768]{2,1,0:T(8,128)S(1)} %bitcast.5), channel_id=1, source_target_pairs={{0,3},{1,2},{2,1},{3,0},{4,7},{5,6},{6,5},{7,4},{8,11},{9,10},{10,... | collective-permute-start | bytes 73736 | tf_op jit(solution)/shard_map/ppermute | solution.py:307
  3.4 0.3 collective-permute-start.3
  3.6 0.2 collective-permute-start.2
  3.8 1.3 %collective-permute-start.1 = (f32[1,8,768]{2,1,0:T(8,128)S(1)}, f32[1,8,768]{2,1,0:T(8,128)S(1)}, u32[]{:S(2)}, u32[]{:S(2)}) collective-permute-start(f32[1,8,768]{2,1,0:T(8,128)S(1)} %bitcast.8), channel_id=1, source_target_pairs={{0,24},{4,28},{8,16},{12,20},{1,25},{5,29},{9,17},{13,21},{2,26},{... | collective-permute-start | bytes 73736 | tf_op jit(solution)/shard_map/ppermute | solution.py:311
  5.1 1.3 %collective-permute-start = (f32[1,8,768]{2,1,0:T(8,128)S(1)}, f32[1,8,768]{2,1,0:T(8,128)S(1)}, u32[]{:S(2)}, u32[]{:S(2)}) collective-permute-start(f32[1,8,768]{2,1,0:T(8,128)S(1)} %bitcast.9), channel_id=1, source_target_pairs={{0,16},{4,20},{8,24},{12,28},{1,17},{5,21},{9,25},{13,29},{2,18},{... | collective-permute-start | bytes 73736 | tf_op jit(solution)/shard_map/ppermute | solution.py:311
  6.4 0.0 collective-permute-done.4
  6.4 0.0 collective-permute-done.3
  6.4 0.0 collective-permute-done.2
  6.5 1.6 %shard_map.69 = (f32[3,144]{1,0:T(4,128)S(1)}, bf16[288,96]{1,0:T(8,128)(2,1)S(1)}, bf16[1,96,3072]{2,1,0:T(8,128)(2,1)S(1)}, bf16[1,32,3072]{2,1,0:T(8,128)(2,1...) custom-call(f32[1,8,768]{2,1,0:T(8,128)S(1)} %bitcast.10, f32[3,8,768]{2,1,0:T(8,128)S(1)} %pad_maximum_fusion.2.there), custom_call_target="tpu_custom_call" | custom-call | flops 500 | bytes 400 | tf_op jit(solution)/shard_map/pallas_call | solution.py:316
  8.0 0.4 collective-permute-done.1
  8.4 3.3 %collective-permute-done = f32[1,8,768]{2,1,0:T(8,128)S(1)} collective-permute-done((f32[1,8,768]{2,1,0:T(8,128)S(1)}, f32[1,8,768]{2,1,0:T(8,128)S(1)}, u32[]{:S(2)}, u32[]{:S(2)}) %collective-permute-start) | collective-permute-done | bytes 24608 | tf_op jit(solution)/shard_map/ppermute | solution.py:311
  11.7 0.0 copy-start
  11.7 0.0 copy-start.1
  11.7 3.1 %collective-permute-start.7 = (f32[2,8,768]{2,1,0:T(8,128)S(1)}, f32[2,8,768]{2,1,0:T(8,128)S(1)}, u32[]{:S(2)}, u32[]{:S(2)}) collective-permute-start(f32[2,8,768]{2,1,0:T(8,128)S(1)} %constant_dynamic-update-slice_fusion.blocks), channel_id=1, source_target_pairs={{16,22},{17,23},{18,20},{19,21},{20,18},{21,19},{22,16},{23,17},{2... | collective-permute-start | bytes 147464 | tf_op jit(solution)/shard_map/ppermute | solution.py:337
  14.8 3.1 %collective-permute-start.6 = (f32[2,8,768]{2,1,0:T(8,128)S(1)}, f32[2,8,768]{2,1,0:T(8,128)S(1)}, u32[]{:S(2)}, u32[]{:S(2)}) collective-permute-start(f32[2,8,768]{2,1,0:T(8,128)S(1)} %constant_dynamic-update-slice_fusion.blocks), channel_id=1, source_target_pairs={{16,20},{17,21},{18,22},{19,23},{20,16},{21,17},{22,18},{23,19},{2... | collective-permute-start | bytes 147464 | tf_op jit(solution)/shard_map/ppermute | solution.py:337
  18.0 2.3 %collective-permute-start.5 = (f32[2,8,768]{2,1,0:T(8,128)S(1)}, f32[2,8,768]{2,1,0:T(8,128)S(1)}, u32[]{:S(2)}, u32[]{:S(2)}) collective-permute-start(f32[2,8,768]{2,1,0:T(8,128)S(1)} %constant_dynamic-update-slice_fusion.blocks), channel_id=1, source_target_pairs={{16,18},{17,19},{18,16},{19,17},{20,22},{21,23},{22,20},{23,21},{2... | collective-permute-start | bytes 147464 | tf_op jit(solution)/shard_map/ppermute | solution.py:337
  20.3 0.0 copy-done
  20.3 0.0 copy-done.1
  20.3 1.7 %shard_map.70 = (bf16[3,96,1536]{2,1,0:T(8,128)(2,1)S(1)}, bf16[3,32,1536]{2,1,0:T(8,128)(2,1)S(1)}, f32[3,1,1536]{2,1,0:T(1,128)S(1)}, f32[32,144]{1,0:T(8,128)S(1)}) custom-call(s32[1,3]{1,0:T(1,128)S(1)} %copy-done, s32[1,3]{1,0:T(1,128)S(1)} %copy-done.1, f32[2,8,768]{2,1,0:T(8,128)S(1)} %constant_dynamic-update-slice_fusion.blocks, ...), custom_call_target="tpu_custom_call" | custom-call | flops 165888000 | bytes 921600 | tf_op jit(solution)/shard_map/pallas_call | solution.py:343
  21.9 0.0 collective-permute-done.7
  22.0 0.0 collective-permute-done.6
  22.0 0.8 %collective-permute-done.5 = f32[2,8,768]{2,1,0:T(8,128)S(1)} collective-permute-done((f32[2,8,768]{2,1,0:T(8,128)S(1)}, f32[2,8,768]{2,1,0:T(8,128)S(1)}, u32[]{:S(2)}, u32[]{:S(2)}) %collective-permute-start.5) | collective-permute-done | bytes 49184 | tf_op jit(solution)/shard_map/ppermute | solution.py:337
  22.8 3.2 %collective-permute-start.8 = (f32[8,8,768]{2,1,0:T(8,128)S(1)}, f32[8,8,768]{2,1,0:T(8,128)S(1)}, u32[]{:S(2)}, u32[]{:S(2)}) collective-permute-start(f32[8,8,768]{2,1,0:T(8,128)S(1)} %pad_maximum_fusion), channel_id=1, source_target_pairs={{0,1},{1,0},{2,3},{3,2},{4,5},{5,4},{6,7},{7,6},{8,9},{9,8},{10,11... | collective-permute-start | bytes 589832 | tf_op jit(solution)/shard_map/ppermute | solution.py:307
  26.1 2.8 %shard_map.71 = (bf16[3,96,1536]{2,1,0:T(8,128)(2,1)S(1)}, bf16[3,32,1536]{2,1,0:T(8,128)(2,1)S(1)}, f32[3,1,1536]{2,1,0:T(1,128)S(1)}, f32[32,144]{1,0:T(8,128)S(1)}) custom-call(s32[1,3]{1,0:T(1,128)S(1)} %copy-done, s32[1,3]{1,0:T(1,128)S(1)} %copy-done.1, ...), custom_call_target="tpu_custom_call", output_to_operand_aliasing={{0}: (5, {}), {1}: (6, {}), {2}: (7, {})} | custom-call | flops 165888000 | bytes 921600 | tf_op jit(solution)/shard_map/pallas_call | solution.py:353
  28.8 0.0 collective-permute-done.8.blocks
  28.9 8.9 %shard_map.72 = (f32[3,1,128]{2,1,0:T(1,128)}, f32[3,1,128]{2,1,0:T(1,128)}) custom-call(s32[1,3]{1,0:T(1,128)S(1)} %copy-done, s32[1,3]{1,0:T(1,128)S(1)} %copy-done.1, f32[8,8,768]{2,1,0:T(8,128)S(1)} %collective-permute-done.8.blocks, f32[3,144]{1,0:T(4,128)S(1)} %get-tuple-element.30.extended_ref, bf16[288,96]{1,0:T(8,128)(2,1)S(1)} %get-tuple-element.26.factors_ref, ...), custom_call_target="tpu_custom_call" | custom-call | flops 884736000 | bytes 4915200 | tf_op jit(solution)/shard_map/pallas_call | solution.py:364
  (5 shorter events, 0.0 us)
Async XLA Ops:
  1.5 4.9 %collective-permute-start.4 = (f32[1,8,768]{2,1,0:T(8,128)S(1)}, f32[1,8,768]{2,1,0:T(8,128)S(1)}, u32[]{:S(2)}, u32[]{:S(2)}) collective-permute-start(f32[1,8,768]{2,1,0:T(8,128)S(1)} %bitcast.5), channel_id=1, source_target_pairs={{0,3},{1,2},{2,1},{3,0},{4,7},{5,6},{6,5},{7,4},{8,11},{9,10},{10,... | collective-permute-start | bytes 73736 | tf_op jit(solution)/shard_map/ppermute | solution.py:307
  3.4 3.1 %collective-permute-start.3 = (f32[1,8,768]{2,1,0:T(8,128)S(1)}, f32[1,8,768]{2,1,0:T(8,128)S(1)}, u32[]{:S(2)}, u32[]{:S(2)}) collective-permute-start(f32[1,8,768]{2,1,0:T(8,128)S(1)} %bitcast.6), channel_id=1, source_target_pairs={{0,2},{1,3},{2,0},{3,1},{4,6},{5,7},{6,4},{7,5},{8,10},{9,11},{10,... | collective-permute-start | bytes 73736 | tf_op jit(solution)/shard_map/ppermute | solution.py:307
  3.6 2.8 %collective-permute-start.2 = (f32[1,8,768]{2,1,0:T(8,128)S(1)}, f32[1,8,768]{2,1,0:T(8,128)S(1)}, u32[]{:S(2)}, u32[]{:S(2)}) collective-permute-start(f32[1,8,768]{2,1,0:T(8,128)S(1)} %bitcast.7), channel_id=1, source_target_pairs={{0,1},{1,0},{2,3},{3,2},{4,5},{5,4},{6,7},{7,6},{8,9},{9,8},{10,11... | collective-permute-start | bytes 73736 | tf_op jit(solution)/shard_map/ppermute | solution.py:307
  3.8 4.6 %collective-permute-start.1 = (f32[1,8,768]{2,1,0:T(8,128)S(1)}, f32[1,8,768]{2,1,0:T(8,128)S(1)}, u32[]{:S(2)}, u32[]{:S(2)}) collective-permute-start(f32[1,8,768]{2,1,0:T(8,128)S(1)} %bitcast.8), channel_id=1, source_target_pairs={{0,24},{4,28},{8,16},{12,20},{1,25},{5,29},{9,17},{13,21},{2,26},{... | collective-permute-start | bytes 73736 | tf_op jit(solution)/shard_map/ppermute | solution.py:311
  5.1 6.6 %collective-permute-start = (f32[1,8,768]{2,1,0:T(8,128)S(1)}, f32[1,8,768]{2,1,0:T(8,128)S(1)}, u32[]{:S(2)}, u32[]{:S(2)}) collective-permute-start(f32[1,8,768]{2,1,0:T(8,128)S(1)} %bitcast.9), channel_id=1, source_target_pairs={{0,16},{4,20},{8,24},{12,28},{1,17},{5,21},{9,25},{13,29},{2,18},{... | collective-permute-start | bytes 73736 | tf_op jit(solution)/shard_map/ppermute | solution.py:311
  11.7 8.6 %copy-start = (s32[1,3]{1,0:T(1,128)S(1)}, s32[1,3]{1,0:T(1,128)}, u32[]{:S(2)}) copy-start(s32[1,3]{1,0:T(1,128)} %upstream.5) | copy-start | bytes 40
  11.7 8.6 %copy-start.1 = (s32[1,3]{1,0:T(1,128)S(1)}, s32[1,3]{1,0:T(1,128)}, u32[]{:S(2)}) copy-start(s32[1,3]{1,0:T(1,128)} %mask.5) | copy-start | bytes 40
  11.7 10.2 %collective-permute-start.7 = (f32[2,8,768]{2,1,0:T(8,128)S(1)}, f32[2,8,768]{2,1,0:T(8,128)S(1)}, u32[]{:S(2)}, u32[]{:S(2)}) collective-permute-start(f32[2,8,768]{2,1,0:T(8,128)S(1)} %constant_dynamic-update-slice_fusion.blocks), channel_id=1, source_target_pairs={{16,22},{17,23},{18,20},{19,21},{20,18},{21,19},{22,16},{23,17},{2... | collective-permute-start | bytes 147464 | tf_op jit(solution)/shard_map/ppermute | solution.py:337
  14.8 7.1 %collective-permute-start.6 = (f32[2,8,768]{2,1,0:T(8,128)S(1)}, f32[2,8,768]{2,1,0:T(8,128)S(1)}, u32[]{:S(2)}, u32[]{:S(2)}) collective-permute-start(f32[2,8,768]{2,1,0:T(8,128)S(1)} %constant_dynamic-update-slice_fusion.blocks), channel_id=1, source_target_pairs={{16,20},{17,21},{18,22},{19,23},{20,16},{21,17},{22,18},{23,19},{2... | collective-permute-start | bytes 147464 | tf_op jit(solution)/shard_map/ppermute | solution.py:337
  18.0 4.8 %collective-permute-start.5 = (f32[2,8,768]{2,1,0:T(8,128)S(1)}, f32[2,8,768]{2,1,0:T(8,128)S(1)}, u32[]{:S(2)}, u32[]{:S(2)}) collective-permute-start(f32[2,8,768]{2,1,0:T(8,128)S(1)} %constant_dynamic-update-slice_fusion.blocks), channel_id=1, source_target_pairs={{16,18},{17,19},{18,16},{19,17},{20,22},{21,23},{22,20},{23,21},{2... | collective-permute-start | bytes 147464 | tf_op jit(solution)/shard_map/ppermute | solution.py:337
  22.8 6.0 %collective-permute-start.8 = (f32[8,8,768]{2,1,0:T(8,128)S(1)}, f32[8,8,768]{2,1,0:T(8,128)S(1)}, u32[]{:S(2)}, u32[]{:S(2)}) collective-permute-start(f32[8,8,768]{2,1,0:T(8,128)S(1)} %pad_maximum_fusion), channel_id=1, source_target_pairs={{0,1},{1,0},{2,3},{3,2},{4,5},{5,4},{6,7},{7,6},{8,9},{9,8},{10,11... | collective-permute-start | bytes 589832 | tf_op jit(solution)/shard_map/ppermute | solution.py:307
